TPU v7x, 256 devices: a whole 4x4x8 slice. The times are simulated.
256 devices in a mesh: head: 4 (over x), inner: 8 (over z_lo, y), outer: 8 (over z_hi, core).
Axes of the slice: x: 4, y: 4, z: 8 (z_hi: 4, z_lo: 2; z = z_hi * 2 + z_lo), core: 2. Of those that a mesh axis runs over, the one named last changes fastest.
Arguments:
- query_heads: bfloat16 [16384, 3072], P(('inner', 'outer', 'head')), may hold values from -256 to 256
- key_heads: bfloat16 [16384, 512], P(('inner', 'outer', 'head')), may hold values from -6 to 6
- value_matrix: bfloat16 [16384, 512], P(('inner', 'outer', 'head')), may hold values from -6 to 6
- out_grad: bfloat16 [16384, 3072], P(('inner', 'outer', 'head')), may hold values from -6 to 6
- segment_ids: int32 [16384], replicated, may hold values from 0 to 63, never falling along the last dimension, each value on 1 to 1792 neighbouring positions
Outputs:
- query_grad: bfloat16 [16384, 3072], P(('inner', 'outer', 'head'))
- key_grad: bfloat16 [16384, 512], P(('inner', 'outer', 'head'))
- value_grad: bfloat16 [16384, 512], P(('inner', 'outer', 'head'))
Inputs may be any that keep to these rules, and one draw needn't show every extreme that they name: `segment_ids`: session ids never fall along the sequence; each session covers at most 1792 positions, and one covers exactly that many.
All inputs are finite; a program needn't handle non-finite values.
Results may differ from a plain program's by a relative error of at most 0.019.
Values may be sent and summed in bfloat16 or wider, within the bound.
A program may use at most 64 MiB of HBM per device.

v0:
```python
import math

import jax
import jax.numpy as jnp
from jax import lax
from jax.sharding import PartitionSpec as P

HEAD_SIZE = 128
QUERY_HEADS = 24
KEY_VALUE_HEADS = 4
WINDOW_DEVICES = 8


NEG_FILL = -1e30


def shifted(value, axis, by):
    size = lax.axis_size(axis)
    pairs = [(i, i + by) for i in range(size) if 0 <= i + by < size]
    return lax.ppermute(value, axis, pairs)


def body(query_heads, key_heads, value_matrix, out_grad, segment_ids):
    query_rows, key_rows, value_rows, grad_rows = (
        lax.all_to_all(query_heads, "head", split_axis=1, concat_axis=0, tiled=True),
        lax.all_to_all(key_heads, "head", split_axis=1, concat_axis=0, tiled=True),
        lax.all_to_all(value_matrix, "head", split_axis=1, concat_axis=0, tiled=True),
        lax.all_to_all(out_grad, "head", split_axis=1, concat_axis=0, tiled=True),
    )
    row_count = query_rows.shape[0]
    kv_local = key_rows.shape[1] // HEAD_SIZE
    group_index = QUERY_HEADS // KEY_VALUE_HEADS
    query_split = query_rows.reshape(row_count, kv_local, group_index, HEAD_SIZE)
    grad_split = grad_rows.reshape(row_count, kv_local, group_index, HEAD_SIZE)
    cycle_place = lax.axis_index(("inner", "outer"))
    score_scale = HEAD_SIZE ** (-0.5)
    width = 2 * kv_local * HEAD_SIZE
    earlier = WINDOW_DEVICES - 1
    window_rows = WINDOW_DEVICES * row_count
    first_row = cycle_place * row_count
    window_first = first_row - earlier * row_count
    query_pos = first_row + jnp.arange(row_count, dtype=jnp.int32)
    query_seg = lax.dynamic_slice_in_dim(segment_ids, first_row, row_count, 0)
    padded_seg = jnp.concatenate([jnp.full((earlier * row_count,), -1, jnp.int32), segment_ids])
    key_list = []
    value_list = []
    for hop in range(earlier, 0, -1):
        far_keys, far_values = shifted((key_rows, value_rows), ("inner", "outer"), hop)
        key_list.append(far_keys)
        value_list.append(far_values)
    key_list.append(key_rows)
    value_list.append(value_rows)
    keys_window = jnp.concatenate(key_list, axis=0)
    values_window = jnp.concatenate(value_list, axis=0)
    block = math.gcd(512, window_rows)
    session_start = jnp.sum((segment_ids < query_seg[0]).astype(jnp.int32))
    low_block = jnp.maximum(session_start - window_first, 0) // block
    high_block = window_rows // block

    def scores_of(key_piece, offset):
        count = key_piece.shape[0]
        key_split = key_piece.reshape(count, kv_local, HEAD_SIZE)
        key_pos = window_first + offset + jnp.arange(count, dtype=jnp.int32)
        key_seg = lax.dynamic_slice_in_dim(padded_seg, first_row + offset, count, 0)
        allowed = (key_pos[None, :] <= query_pos[:, None]) & (
            key_seg[None, :] == query_seg[:, None]
        )
        allowed = allowed[:, None, None, :]
        scores = (
            jnp.einsum("rkgd,ckd->rkgc", query_split, key_split, preferred_element_type=jnp.float32)
            * score_scale
        )
        return (key_split, allowed, jnp.where(allowed, scores, NEG_FILL))

    def prob_grads_of(value_piece):
        value_split = value_piece.reshape(value_piece.shape[0], kv_local, HEAD_SIZE)
        return jnp.einsum(
            "rkgd,ckd->rkgc", grad_split, value_split, preferred_element_type=jnp.float32
        )

    def sweep(step_fn, init):

        def loop_body(number, carry):
            offset = number * block
            pieces = (
                lax.dynamic_slice_in_dim(keys_window, offset, block, 0),
                lax.dynamic_slice_in_dim(values_window, offset, block, 0),
            )
            return step_fn(carry, pieces, offset)

        return lax.fori_loop(low_block, high_block, loop_body, init)

    def stats_step(carry, pieces, offset):
        row_top, row_total, row_cross = carry
        key_split, allowed, masked = scores_of(pieces[0], offset)
        new_top = jnp.maximum(row_top, jnp.max(masked, axis=-1))
        probs = jnp.where(allowed, jnp.exp(masked - new_top[..., None]), 0.0)
        fade = jnp.exp(row_top - new_top)
        prob_grads = prob_grads_of(pieces[1])
        return (
            new_top,
            row_total * fade + jnp.sum(probs, axis=-1),
            row_cross * fade + jnp.sum(probs * prob_grads, axis=-1),
        )

    stats_shape = (row_count, kv_local, group_index)
    stats_init = (
        jnp.full(stats_shape, NEG_FILL, jnp.float32),
        jnp.zeros(stats_shape, jnp.float32),
        jnp.zeros(stats_shape, jnp.float32),
    )
    row_top, row_total, row_cross = sweep(stats_step, stats_init)
    lse = row_top + jnp.log(row_total)
    delta = row_cross / row_total

    def grad_step(carry, pieces, offset):
        query_acc, pair_acc = carry
        key_split, allowed, masked = scores_of(pieces[0], offset)
        count = key_split.shape[0]
        probs = jnp.where(allowed, jnp.exp(masked - lse[..., None]), 0.0)
        prob_grads = prob_grads_of(pieces[1])
        score_grads = (probs * (prob_grads - delta[..., None])).astype(jnp.bfloat16)
        probs_half = probs.astype(jnp.bfloat16)
        query_acc = query_acc + score_scale * jnp.einsum(
            "rkgc,ckd->rkgd", score_grads, key_split, preferred_element_type=jnp.float32
        )
        key_part = score_scale * jnp.einsum(
            "rkgc,rkgd->ckd", score_grads, query_split, preferred_element_type=jnp.float32
        )
        value_part = jnp.einsum(
            "rkgc,rkgd->ckd", probs_half, grad_split, preferred_element_type=jnp.float32
        )
        fresh = jnp.concatenate(
            [
                key_part.reshape(count, kv_local * HEAD_SIZE),
                value_part.reshape(count, kv_local * HEAD_SIZE),
            ],
            axis=1,
        )
        previous = lax.dynamic_slice_in_dim(pair_acc, offset, count, 0)
        return (query_acc, lax.dynamic_update_slice_in_dim(pair_acc, previous + fresh, offset, 0))

    grads_init = (
        jnp.zeros((row_count, kv_local, group_index, HEAD_SIZE), jnp.float32),
        jnp.zeros((window_rows, width), jnp.float32),
    )
    query_acc, pair_acc = sweep(grad_step, grads_init)
    shares = pair_acc[earlier * row_count :]
    for hop in range(1, WINDOW_DEVICES):
        low = (earlier - hop) * row_count
        arrived = shifted(pair_acc[low : low + row_count], ("inner", "outer"), -hop)
        shares = shares + arrived
    shares_half = shares.astype(jnp.bfloat16)
    key_out = shares_half[:, : kv_local * HEAD_SIZE]
    value_out = shares_half[:, kv_local * HEAD_SIZE :]
    query_out = query_acc.astype(jnp.bfloat16).reshape(
        row_count, kv_local * group_index * HEAD_SIZE
    )
    query_grad, key_grad, value_grad = (
        lax.all_to_all(query_out, "head", split_axis=0, concat_axis=1, tiled=True),
        lax.all_to_all(key_out, "head", split_axis=0, concat_axis=1, tiled=True),
        lax.all_to_all(value_out, "head", split_axis=0, concat_axis=1, tiled=True),
    )
    return (query_grad, key_grad, value_grad)


def solution(mesh):
    in_specs = (
        P(("inner", "outer", "head"), None),
        P(("inner", "outer", "head"), None),
        P(("inner", "outer", "head"), None),
        P(("inner", "outer", "head"), None),
        P(),
    )
    out_specs = (
        P(("inner", "outer", "head"), None),
        P(("inner", "outer", "head"), None),
        P(("inner", "outer", "head"), None),
    )
    return jax.shard_map(body, mesh=mesh, in_specs=in_specs, out_specs=out_specs, check_vma=False)
```

profile of v0, /device:TPU:32, one launch (start us, length us, event | category | flops | bytes accessed | tf_op | source)
XLA Modules:
  0.0 238.3 jit_solution(13358350098032915968)
XLA Ops:
  2.1 4.3 %all-to-all-start = ((bf16[64,4,128]{2,0,1:T(8,128)(2,1)}), bf16[64,4,128]{2,0,1:T(8,128)(2,1)S(1)}, u32[]{:S(2)}, u32[]{:S(2)}) async-start(bf16[64,4,128]{2,0,1:T(8,128)(2,1)} %copy_bitcast_fusion.5), calls=%async_computation | async-start | bytes 131072 | tf_op jit(solution)/shard_map/all_to_all | solution.py:26
  6.4 1.5 copy_bitcast_fusion.4
  9.2 2.9 %all-to-all-done = bf16[64,4,128]{2,0,1:T(8,128)(2,1)S(1)} async-done(((bf16[64,4,128]{2,0,1:T(8,128)(2,1)}), bf16[64,4,128]{2,0,1:T(8,128)(2,1)S(1)}, u32[]{:S(2)}, u32[]{:S(2)}) %all-to-all-start) | async-done | bytes 65568 | tf_op jit(solution)/shard_map/all_to_all | solution.py:26
  12.0 3.3 %all-to-all-start.2 = ((bf16[64,4,128]{2,0,1:T(8,128)(2,1)}), bf16[64,4,128]{2,0,1:T(8,128)(2,1)S(1)}, u32[]{:S(2)}, u32[]{:S(2)}) async-start(bf16[64,4,128]{2,0,1:T(8,128)(2,1)} %copy_bitcast_fusion.4), calls=%async_computation.2 | async-start | bytes 131072 | tf_op jit(solution)/shard_map/all_to_all | solution.py:27
  15.3 5.3 %collective-permute-start = (bf16[256,128]{1,0:T(8,128)(2,1)S(1)}, bf16[256,128]{1,0:T(8,128)(2,1)S(1)}, u32[]{:S(2)}, u32[]{:S(2)}) collective-permute-start(bf16[256,128]{1,0:T(8,128)(2,1)S(1)} %bitcast.243), channel_id=1, source_target_pairs={{0,7},{1,8},{2,9},{3,10},{4,11},{5,12},{6,13},{7,14},{8,15},{9,16}... | collective-permute-start | bytes 196616 | tf_op jit(solution)/shard_map/ppermute | solution.py:20
  20.7 2.1 convert_reduce_fusion
  24.3 1.8 copy.96
  26.1 1.8 copy.95
  27.8 4.4 %collective-permute-start.1 = (bf16[256,128]{1,0:T(8,128)(2,1)S(1)}, bf16[256,128]{1,0:T(8,128)(2,1)S(1)}, u32[]{:S(2)}, u32[]{:S(2)}) collective-permute-start(bf16[256,128]{1,0:T(8,128)(2,1)S(1)} %bitcast.244), channel_id=1, source_target_pairs={{0,6},{1,7},{2,8},{3,9},{4,10},{5,11},{6,12},{7,13},{8,14},{9,15},... | collective-permute-start | bytes 196616 | tf_op jit(solution)/shard_map/ppermute | solution.py:20
  32.2 4.9 %collective-permute-start.2 = (bf16[256,128]{1,0:T(8,128)(2,1)S(1)}, bf16[256,128]{1,0:T(8,128)(2,1)S(1)}, u32[]{:S(2)}, u32[]{:S(2)}) collective-permute-start(bf16[256,128]{1,0:T(8,128)(2,1)S(1)} %bitcast.245), channel_id=1, source_target_pairs={{0,5},{1,6},{2,7},{3,8},{4,9},{5,10},{6,11},{7,12},{8,13},{9,14},{... | collective-permute-start | bytes 196616 | tf_op jit(solution)/shard_map/ppermute | solution.py:20
  37.1 6.4 %collective-permute-start.3 = (bf16[256,128]{1,0:T(8,128)(2,1)S(1)}, bf16[256,128]{1,0:T(8,128)(2,1)S(1)}, u32[]{:S(2)}, u32[]{:S(2)}) collective-permute-start(bf16[256,128]{1,0:T(8,128)(2,1)S(1)} %bitcast.246), channel_id=1, source_target_pairs={{0,4},{1,5},{2,6},{3,7},{4,8},{5,9},{6,10},{7,11},{8,12},{9,13},{1... | collective-permute-start | bytes 196616 | tf_op jit(solution)/shard_map/ppermute | solution.py:20
  43.5 1.9 collective-permute-start.4
  45.5 3.4 %collective-permute-start.5 = (bf16[256,128]{1,0:T(8,128)(2,1)S(1)}, bf16[256,128]{1,0:T(8,128)(2,1)S(1)}, u32[]{:S(2)}, u32[]{:S(2)}) collective-permute-start(bf16[256,128]{1,0:T(8,128)(2,1)S(1)} %bitcast.248), channel_id=1, source_target_pairs={{0,2},{1,3},{2,4},{3,5},{4,6},{5,7},{6,8},{7,9},{8,10},{9,11},{10,... | collective-permute-start | bytes 196616 | tf_op jit(solution)/shard_map/ppermute | solution.py:20
  49.5 4.8 %collective-permute-start.6 = (bf16[256,128]{1,0:T(8,128)(2,1)S(1)}, bf16[256,128]{1,0:T(8,128)(2,1)S(1)}, u32[]{:S(2)}, u32[]{:S(2)}) collective-permute-start(bf16[256,128]{1,0:T(8,128)(2,1)S(1)} %bitcast.249), channel_id=1, source_target_pairs={{0,1},{1,2},{2,3},{3,4},{4,5},{5,6},{6,7},{7,8},{8,9},{9,10},{10,1... | collective-permute-start | bytes 196616 | tf_op jit(solution)/shard_map/ppermute | solution.py:20
  54.9 4.8 %all-to-all-start.1 = ((bf16[64,4,768]{2,0,1:T(8,128)(2,1)}), bf16[64,4,768]{2,0,1:T(8,128)(2,1)S(1)}, u32[]{:S(2)}, u32[]{:S(2)}) async-start(bf16[64,4,768]{2,0,1:T(8,128)(2,1)} %bitcast.166), calls=%async_computation.1 | async-start | bytes 786432 | tf_op jit(solution)/shard_map/all_to_all | solution.py:25
  59.7 2.7 %collective-permute-start.7 = (bf16[256,128]{1,0:T(8,128)(2,1)S(1)}, bf16[256,128]{1,0:T(8,128)(2,1)S(1)}, u32[]{:S(2)}, u32[]{:S(2)}) collective-permute-start(bf16[256,128]{1,0:T(8,128)(2,1)S(1)} %bitcast.235), channel_id=1, source_target_pairs={{0,7},{1,8},{2,9},{3,10},{4,11},{5,12},{6,13},{7,14},{8,15},{9,16}... | collective-permute-start | bytes 196616 | tf_op jit(solution)/shard_map/ppermute | solution.py:20
  63.0 2.6 %collective-permute-start.8 = (bf16[256,128]{1,0:T(8,128)(2,1)S(1)}, bf16[256,128]{1,0:T(8,128)(2,1)S(1)}, u32[]{:S(2)}, u32[]{:S(2)}) collective-permute-start(bf16[256,128]{1,0:T(8,128)(2,1)S(1)} %bitcast.236), channel_id=1, source_target_pairs={{0,6},{1,7},{2,8},{3,9},{4,10},{5,11},{6,12},{7,13},{8,14},{9,15},... | collective-permute-start | bytes 196616 | tf_op jit(solution)/shard_map/ppermute | solution.py:20
  66.3 2.7 %collective-permute-start.9 = (bf16[256,128]{1,0:T(8,128)(2,1)S(1)}, bf16[256,128]{1,0:T(8,128)(2,1)S(1)}, u32[]{:S(2)}, u32[]{:S(2)}) collective-permute-start(bf16[256,128]{1,0:T(8,128)(2,1)S(1)} %bitcast.237), channel_id=1, source_target_pairs={{0,5},{1,6},{2,7},{3,8},{4,9},{5,10},{6,11},{7,12},{8,13},{9,14},{... | collective-permute-start | bytes 196616 | tf_op jit(solution)/shard_map/ppermute | solution.py:20
  69.6 4.3 %collective-permute-start.10 = (bf16[256,128]{1,0:T(8,128)(2,1)S(1)}, bf16[256,128]{1,0:T(8,128)(2,1)S(1)}, u32[]{:S(2)}, u32[]{:S(2)}) collective-permute-start(bf16[256,128]{1,0:T(8,128)(2,1)S(1)} %bitcast.238), channel_id=1, source_target_pairs={{0,4},{1,5},{2,6},{3,7},{4,8},{5,9},{6,10},{7,11},{8,12},{9,13},{1... | collective-permute-start | bytes 196616 | tf_op jit(solution)/shard_map/ppermute | solution.py:20
  74.5 1.9 collective-permute-start.11
  77.7 2.8 %collective-permute-start.12 = (bf16[256,128]{1,0:T(8,128)(2,1)S(1)}, bf16[256,128]{1,0:T(8,128)(2,1)S(1)}, u32[]{:S(2)}, u32[]{:S(2)}) collective-permute-start(bf16[256,128]{1,0:T(8,128)(2,1)S(1)} %bitcast.240), channel_id=1, source_target_pairs={{0,2},{1,3},{2,4},{3,5},{4,6},{5,7},{6,8},{7,9},{8,10},{9,11},{10,... | collective-permute-start | bytes 196616 | tf_op jit(solution)/shard_map/ppermute | solution.py:20
  80.6 3.4 %collective-permute-start.13 = (bf16[256,128]{1,0:T(8,128)(2,1)S(1)}, bf16[256,128]{1,0:T(8,128)(2,1)S(1)}, u32[]{:S(2)}, u32[]{:S(2)}) collective-permute-start(bf16[256,128]{1,0:T(8,128)(2,1)S(1)} %bitcast.241), channel_id=1, source_target_pairs={{0,1},{1,2},{2,3},{3,4},{4,5},{5,6},{6,7},{7,8},{8,9},{9,10},{10,1... | collective-permute-start | bytes 196616 | tf_op jit(solution)/shard_map/ppermute | solution.py:20
  84.1 1.5 collective-permute-done.11
  85.7 4.5 %all-to-all-start.3 = ((bf16[64,4,768]{2,0,1:T(8,128)(2,1)}), bf16[64,4,768]{2,0,1:T(8,128)(2,1)S(1)}, u32[]{:S(2)}, u32[]{:S(2)}) async-start(bf16[64,4,768]{2,0,1:T(8,128)(2,1)} %bitcast.165), calls=%async_computation.3 | async-start | bytes 786432 | tf_op jit(solution)/shard_map/all_to_all | solution.py:28
  92.1 5.4 %all-to-all-done.3 = bf16[64,4,768]{2,0,1:T(8,128)(2,1)S(1)} async-done(((bf16[64,4,768]{2,0,1:T(8,128)(2,1)}), bf16[64,4,768]{2,0,1:T(8,128)(2,1)S(1)}, u32[]{:S(2)}, u32[]{:S(2)}) %all-to-all-start.3) | async-done | bytes 393248 | tf_op jit(solution)/shard_map/all_to_all | solution.py:28
  98.4 15.3 %while.30 = (s32[]{:T(128)}, f32[256,1,6]{0,2,1:T(8,128)S(1)}, f32[256,1,6]{0,2,1:T(8,128)S(1)}, f32[256,1,6]{0,2,1:T(8,128)S(1)}, s32[]{:T(128)}, /*index=5*/s3...) while((s32[]{:T(128)}, f32[256,1,6]{0,2,1:T(8,128)S(1)}, ...), condition=%wide.region_5.6_spmd.clone.clone, body=%wide.region_1.5_spmd.clone.clone.sunk | while | flops 414061824 | bytes 11136281 | solution.py:91
  98.7 1.5 fusion.93
  102.6 1.5 fusion.93
  106.4 1.5 fusion.93
  110.2 1.5 fusion.93
  113.7 1.5 broadcast_in_dim.56.clone
  116.1 51.7 %while.31 = (s32[]{:T(128)}, f32[256,1,6,128]{0,3,2,1:T(8,128)}, f32[2048,256]{1,0:T(8,128)}, bf16[2048,128]{1,0:T(8,128)(2,1)}, s32[]{:T(128)}, /*index=5*/s32[...) while((s32[]{:T(128)}, f32[256,1,6,128]{0,3,2,1:T(8,128)}, ...), condition=%wide.region_7.8_spmd.clone.clone, body=%wide.region_6.7_spmd.clone.clone.sunk | while | flops 1017185024 | bytes 31751580 | solution.py:91
  117.1 1.5 fusion.106
  118.6 2.1 fusion.107
  121.3 1.8 fusion.109
  126.5 2.5 %fusion.108 = f32[256,1,6,128]{0,3,2,1:T(8,128)} fusion(f32[256,1,6,128]{0,3,2,1:T(8,128)} %get-tuple-element.625, bf16[256,1,6,512]{0,3,2,1:T(8,128)(2,1)S(1)} %fusion.107, bf16[2048,128]{1,0:T(8,128)(2,1)} %get-tuple-element.645, s32[]{:T(128)S(6)} %select_n.119), kind=kOutput, calls=%fused_computation.41.clone.1 | convolution fusion | flops 201719808 | bytes 3276804 | tf_op jit(solution)/shard_map/while/body/rkgc,ckd->rkgd/dot_general | solution.py:124
  130.1 1.5 fusion.106
  131.5 2.1 fusion.107
  134.2 1.8 fusion.109
  139.4 2.5 %fusion.108 = f32[256,1,6,128]{0,3,2,1:T(8,128)} fusion(f32[256,1,6,128]{0,3,2,1:T(8,128)} %get-tuple-element.625, bf16[256,1,6,512]{0,3,2,1:T(8,128)(2,1)S(1)} %fusion.107, bf16[2048,128]{1,0:T(8,128)(2,1)} %get-tuple-element.645, s32[]{:T(128)S(6)} %select_n.119), kind=kOutput, calls=%fused_computation.41.clone.1 | convolution fusion | flops 201719808 | bytes 3276804 | tf_op jit(solution)/shard_map/while/body/rkgc,ckd->rkgd/dot_general | solution.py:124
  143.0 1.5 fusion.106
  144.5 2.1 fusion.107
  147.2 1.8 fusion.109
  152.3 2.5 %fusion.108 = f32[256,1,6,128]{0,3,2,1:T(8,128)} fusion(f32[256,1,6,128]{0,3,2,1:T(8,128)} %get-tuple-element.625, bf16[256,1,6,512]{0,3,2,1:T(8,128)(2,1)S(1)} %fusion.107, bf16[2048,128]{1,0:T(8,128)(2,1)} %get-tuple-element.645, s32[]{:T(128)S(6)} %select_n.119), kind=kOutput, calls=%fused_computation.41.clone.1 | convolution fusion | flops 201719808 | bytes 3276804 | tf_op jit(solution)/shard_map/while/body/rkgc,ckd->rkgd/dot_general | solution.py:124
  155.9 1.5 fusion.106
  157.4 2.1 fusion.107
  160.1 1.8 fusion.109
  165.3 2.5 %fusion.108 = f32[256,1,6,128]{0,3,2,1:T(8,128)} fusion(f32[256,1,6,128]{0,3,2,1:T(8,128)} %get-tuple-element.625, bf16[256,1,6,512]{0,3,2,1:T(8,128)(2,1)S(1)} %fusion.107, bf16[2048,128]{1,0:T(8,128)(2,1)} %get-tuple-element.645, s32[]{:T(128)S(6)} %select_n.119), kind=kOutput, calls=%fused_computation.41.clone.1 | convolution fusion | flops 201719808 | bytes 3276804 | tf_op jit(solution)/shard_map/while/body/rkgc,ckd->rkgd/dot_general | solution.py:124
  167.8 1.6 fusion.64
  169.4 1.9 collective-permute-start.14
  171.4 1.9 collective-permute-start.15
  173.3 1.9 collective-permute-start.16
  175.2 1.9 collective-permute-start.17
  177.2 1.9 collective-permute-start.18
  179.1 1.9 collective-permute-start.19
  181.0 2.7 %collective-permute-done.15 = f32[256,256]{1,0:T(8,128)S(1)} collective-permute-done((f32[256,256]{1,0:T(8,128)S(1)}, f32[256,256]{1,0:T(8,128)S(1)}, u32[]{:S(2)}, u32[]{:S(2)}) %collective-permute-start.15) | collective-permute-done | bytes 262176 | tf_op jit(solution)/shard_map/ppermute | solution.py:20
  183.8 23.6 %collective-permute-start.20 = (f32[256,256]{1,0:T(8,128)S(1)}, f32[256,256]{1,0:T(8,128)}, u32[]{:S(2)}, u32[]{:S(2)}) collective-permute-start(f32[256,256]{1,0:T(8,128)S(1)} %get-tuple-element.390), channel_id=1, source_target_pairs={{7,0},{8,1},{9,2},{10,3},{11,4},{12,5},{13,6},{14,7},{15,8},{16,9}... | collective-permute-start | bytes 786440 | tf_op jit(solution)/shard_map/ppermute | solution.py:20
  208.9 3.5 %all-to-all-start.4 = ((bf16[4,64,768]{2,1,0:T(8,128)(2,1)}), bf16[4,64,768]{2,1,0:T(8,128)(2,1)S(1)}, u32[]{:S(2)}, u32[]{:S(2)}) async-start(bf16[4,64,768]{2,1,0:T(8,128)(2,1)} %all_to_all.108), calls=%async_computation.4 | async-start | bytes 786432 | tf_op jit(solution)/shard_map/all_to_all | solution.py:160
  212.4 1.3 add_convert_fusion
  214.4 5.5 %all-to-all-done.4 = bf16[4,64,768]{2,1,0:T(8,128)(2,1)S(1)} async-done(((bf16[4,64,768]{2,1,0:T(8,128)(2,1)}), bf16[4,64,768]{2,1,0:T(8,128)(2,1)S(1)}, u32[]{:S(2)}, u32[]{:S(2)}) %all-to-all-start.4) | async-done | bytes 393248 | tf_op jit(solution)/shard_map/all_to_all | solution.py:160
  219.9 3.3 %all-to-all-start.6 = ((bf16[4,64,128]{2,1,0:T(8,128)(2,1)}), bf16[4,64,128]{2,1,0:T(8,128)(2,1)S(1)}, u32[]{:S(2)}, u32[]{:S(2)}) async-start(bf16[4,64,128]{2,1,0:T(8,128)(2,1)} %bitcast.12), calls=%async_computation.6 | async-start | bytes 131072 | tf_op jit(solution)/shard_map/all_to_all | solution.py:162
  224.0 4.8 %all-to-all-done.6 = bf16[4,64,128]{2,1,0:T(8,128)(2,1)S(1)} async-done(((bf16[4,64,128]{2,1,0:T(8,128)(2,1)}), bf16[4,64,128]{2,1,0:T(8,128)(2,1)S(1)}, u32[]{:S(2)}, u32[]{:S(2)}) %all-to-all-start.6) | async-done | bytes 65568 | tf_op jit(solution)/shard_map/all_to_all | solution.py:162
  228.8 3.3 %all-to-all-start.5 = ((bf16[4,64,128]{2,1,0:T(8,128)(2,1)}), bf16[4,64,128]{2,1,0:T(8,128)(2,1)S(1)}, u32[]{:S(2)}, u32[]{:S(2)}) async-start(bf16[4,64,128]{2,1,0:T(8,128)(2,1)} %bitcast.10), calls=%async_computation.5 | async-start | bytes 131072 | tf_op jit(solution)/shard_map/all_to_all | solution.py:161
  232.7 5.0 %all-to-all-done.5 = bf16[4,64,128]{2,1,0:T(8,128)(2,1)S(1)} async-done(((bf16[4,64,128]{2,1,0:T(8,128)(2,1)}), bf16[4,64,128]{2,1,0:T(8,128)(2,1)S(1)}, u32[]{:S(2)}, u32[]{:S(2)}) %all-to-all-start.5) | async-done | bytes 65568 | tf_op jit(solution)/shard_map/all_to_all | solution.py:161
  (171 shorter events, 45.4 us)
Async XLA Ops:
  0.6 0.8 copy-start
  2.1 9.9 %all-to-all-start = ((bf16[64,4,128]{2,0,1:T(8,128)(2,1)}), bf16[64,4,128]{2,0,1:T(8,128)(2,1)S(1)}, u32[]{:S(2)}, u32[]{:S(2)}) async-start(bf16[64,4,128]{2,0,1:T(8,128)(2,1)} %copy_bitcast_fusion.5), calls=%async_computation | async-start | bytes 131072 | tf_op jit(solution)/shard_map/all_to_all | solution.py:26
  12.0 42.9 %all-to-all-start.2 = ((bf16[64,4,128]{2,0,1:T(8,128)(2,1)}), bf16[64,4,128]{2,0,1:T(8,128)(2,1)S(1)}, u32[]{:S(2)}, u32[]{:S(2)}) async-start(bf16[64,4,128]{2,0,1:T(8,128)(2,1)} %copy_bitcast_fusion.4), calls=%async_computation.2 | async-start | bytes 131072 | tf_op jit(solution)/shard_map/all_to_all | solution.py:27
  15.3 30.1 %collective-permute-start = (bf16[256,128]{1,0:T(8,128)(2,1)S(1)}, bf16[256,128]{1,0:T(8,128)(2,1)S(1)}, u32[]{:S(2)}, u32[]{:S(2)}) collective-permute-start(bf16[256,128]{1,0:T(8,128)(2,1)S(1)} %bitcast.243), channel_id=1, source_target_pairs={{0,7},{1,8},{2,9},{3,10},{4,11},{5,12},{6,13},{7,14},{8,15},{9,16}... | collective-permute-start | bytes 196616 | tf_op jit(solution)/shard_map/ppermute | solution.py:20
  27.8 21.6 %collective-permute-start.1 = (bf16[256,128]{1,0:T(8,128)(2,1)S(1)}, bf16[256,128]{1,0:T(8,128)(2,1)S(1)}, u32[]{:S(2)}, u32[]{:S(2)}) collective-permute-start(bf16[256,128]{1,0:T(8,128)(2,1)S(1)} %bitcast.244), channel_id=1, source_target_pairs={{0,6},{1,7},{2,8},{3,9},{4,10},{5,11},{6,12},{7,13},{8,14},{9,15},... | collective-permute-start | bytes 196616 | tf_op jit(solution)/shard_map/ppermute | solution.py:20
  32.2 27.5 %collective-permute-start.2 = (bf16[256,128]{1,0:T(8,128)(2,1)S(1)}, bf16[256,128]{1,0:T(8,128)(2,1)S(1)}, u32[]{:S(2)}, u32[]{:S(2)}) collective-permute-start(bf16[256,128]{1,0:T(8,128)(2,1)S(1)} %bitcast.245), channel_id=1, source_target_pairs={{0,5},{1,6},{2,7},{3,8},{4,9},{5,10},{6,11},{7,12},{8,13},{9,14},{... | collective-permute-start | bytes 196616 | tf_op jit(solution)/shard_map/ppermute | solution.py:20
  37.1 25.9 %collective-permute-start.3 = (bf16[256,128]{1,0:T(8,128)(2,1)S(1)}, bf16[256,128]{1,0:T(8,128)(2,1)S(1)}, u32[]{:S(2)}, u32[]{:S(2)}) collective-permute-start(bf16[256,128]{1,0:T(8,128)(2,1)S(1)} %bitcast.246), channel_id=1, source_target_pairs={{0,4},{1,5},{2,6},{3,7},{4,8},{5,9},{6,10},{7,11},{8,12},{9,13},{1... | collective-permute-start | bytes 196616 | tf_op jit(solution)/shard_map/ppermute | solution.py:20
  43.5 22.7 %collective-permute-start.4 = (bf16[256,128]{1,0:T(8,128)(2,1)S(1)}, bf16[256,128]{1,0:T(8,128)(2,1)S(1)}, u32[]{:S(2)}, u32[]{:S(2)}) collective-permute-start(bf16[256,128]{1,0:T(8,128)(2,1)S(1)} %bitcast.247), channel_id=1, source_target_pairs={{0,3},{1,4},{2,5},{3,6},{4,7},{5,8},{6,9},{7,10},{8,11},{9,12},{10... | collective-permute-start | bytes 196616 | tf_op jit(solution)/shard_map/ppermute | solution.py:20
  45.5 24.1 %collective-permute-start.5 = (bf16[256,128]{1,0:T(8,128)(2,1)S(1)}, bf16[256,128]{1,0:T(8,128)(2,1)S(1)}, u32[]{:S(2)}, u32[]{:S(2)}) collective-permute-start(bf16[256,128]{1,0:T(8,128)(2,1)S(1)} %bitcast.248), channel_id=1, source_target_pairs={{0,2},{1,3},{2,4},{3,5},{4,6},{5,7},{6,8},{7,9},{8,10},{9,11},{10,... | collective-permute-start | bytes 196616 | tf_op jit(solution)/shard_map/ppermute | solution.py:20
  49.5 25.1 %collective-permute-start.6 = (bf16[256,128]{1,0:T(8,128)(2,1)S(1)}, bf16[256,128]{1,0:T(8,128)(2,1)S(1)}, u32[]{:S(2)}, u32[]{:S(2)}) collective-permute-start(bf16[256,128]{1,0:T(8,128)(2,1)S(1)} %bitcast.249), channel_id=1, source_target_pairs={{0,1},{1,2},{2,3},{3,4},{4,5},{5,6},{6,7},{7,8},{8,9},{9,10},{10,1... | collective-permute-start | bytes 196616 | tf_op jit(solution)/shard_map/ppermute | solution.py:20
  54.9 30.7 %all-to-all-start.1 = ((bf16[64,4,768]{2,0,1:T(8,128)(2,1)}), bf16[64,4,768]{2,0,1:T(8,128)(2,1)S(1)}, u32[]{:S(2)}, u32[]{:S(2)}) async-start(bf16[64,4,768]{2,0,1:T(8,128)(2,1)} %bitcast.166), calls=%async_computation.1 | async-start | bytes 786432 | tf_op jit(solution)/shard_map/all_to_all | solution.py:25
  59.7 18.0 %collective-permute-start.7 = (bf16[256,128]{1,0:T(8,128)(2,1)S(1)}, bf16[256,128]{1,0:T(8,128)(2,1)S(1)}, u32[]{:S(2)}, u32[]{:S(2)}) collective-permute-start(bf16[256,128]{1,0:T(8,128)(2,1)S(1)} %bitcast.235), channel_id=1, source_target_pairs={{0,7},{1,8},{2,9},{3,10},{4,11},{5,12},{6,13},{7,14},{8,15},{9,16}... | collective-permute-start | bytes 196616 | tf_op jit(solution)/shard_map/ppermute | solution.py:20
  63.0 17.5 %collective-permute-start.8 = (bf16[256,128]{1,0:T(8,128)(2,1)S(1)}, bf16[256,128]{1,0:T(8,128)(2,1)S(1)}, u32[]{:S(2)}, u32[]{:S(2)}) collective-permute-start(bf16[256,128]{1,0:T(8,128)(2,1)S(1)} %bitcast.236), channel_id=1, source_target_pairs={{0,6},{1,7},{2,8},{3,9},{4,10},{5,11},{6,12},{7,13},{8,14},{9,15},... | collective-permute-start | bytes 196616 | tf_op jit(solution)/shard_map/ppermute | solution.py:20
  66.3 17.8 %collective-permute-start.9 = (bf16[256,128]{1,0:T(8,128)(2,1)S(1)}, bf16[256,128]{1,0:T(8,128)(2,1)S(1)}, u32[]{:S(2)}, u32[]{:S(2)}) collective-permute-start(bf16[256,128]{1,0:T(8,128)(2,1)S(1)} %bitcast.237), channel_id=1, source_target_pairs={{0,5},{1,6},{2,7},{3,8},{4,9},{5,10},{6,11},{7,12},{8,13},{9,14},{... | collective-permute-start | bytes 196616 | tf_op jit(solution)/shard_map/ppermute | solution.py:20
  69.6 14.5 %collective-permute-start.10 = (bf16[256,128]{1,0:T(8,128)(2,1)S(1)}, bf16[256,128]{1,0:T(8,128)(2,1)S(1)}, u32[]{:S(2)}, u32[]{:S(2)}) collective-permute-start(bf16[256,128]{1,0:T(8,128)(2,1)S(1)} %bitcast.238), channel_id=1, source_target_pairs={{0,4},{1,5},{2,6},{3,7},{4,8},{5,9},{6,10},{7,11},{8,12},{9,13},{1... | collective-permute-start | bytes 196616 | tf_op jit(solution)/shard_map/ppermute | solution.py:20
  74.5 11.1 %collective-permute-start.11 = (bf16[256,128]{1,0:T(8,128)(2,1)S(1)}, bf16[256,128]{1,0:T(8,128)(2,1)S(1)}, u32[]{:S(2)}, u32[]{:S(2)}) collective-permute-start(bf16[256,128]{1,0:T(8,128)(2,1)S(1)} %bitcast.239), channel_id=1, source_target_pairs={{0,3},{1,4},{2,5},{3,6},{4,7},{5,8},{6,9},{7,10},{8,11},{9,12},{10... | collective-permute-start | bytes 196616 | tf_op jit(solution)/shard_map/ppermute | solution.py:20
  77.7 12.5 %collective-permute-start.12 = (bf16[256,128]{1,0:T(8,128)(2,1)S(1)}, bf16[256,128]{1,0:T(8,128)(2,1)S(1)}, u32[]{:S(2)}, u32[]{:S(2)}) collective-permute-start(bf16[256,128]{1,0:T(8,128)(2,1)S(1)} %bitcast.240), channel_id=1, source_target_pairs={{0,2},{1,3},{2,4},{3,5},{4,6},{5,7},{6,8},{7,9},{8,10},{9,11},{10,... | collective-permute-start | bytes 196616 | tf_op jit(solution)/shard_map/ppermute | solution.py:20
  80.6 10.7 %collective-permute-start.13 = (bf16[256,128]{1,0:T(8,128)(2,1)S(1)}, bf16[256,128]{1,0:T(8,128)(2,1)S(1)}, u32[]{:S(2)}, u32[]{:S(2)}) collective-permute-start(bf16[256,128]{1,0:T(8,128)(2,1)S(1)} %bitcast.241), channel_id=1, source_target_pairs={{0,1},{1,2},{2,3},{3,4},{4,5},{5,6},{6,7},{7,8},{8,9},{9,10},{10,1... | collective-permute-start | bytes 196616 | tf_op jit(solution)/shard_map/ppermute | solution.py:20
  85.7 11.9 %all-to-all-start.3 = ((bf16[64,4,768]{2,0,1:T(8,128)(2,1)}), bf16[64,4,768]{2,0,1:T(8,128)(2,1)S(1)}, u32[]{:S(2)}, u32[]{:S(2)}) async-start(bf16[64,4,768]{2,0,1:T(8,128)(2,1)} %bitcast.165), calls=%async_computation.3 | async-start | bytes 786432 | tf_op jit(solution)/shard_map/all_to_all | solution.py:28
  116.1 0.8 copy-start.4
  116.1 5.2 %copy-start.2 = (bf16[256,1,6,128]{0,3,2,1:T(8,128)(2,1)}, bf16[256,1,6,128]{0,3,2,1:T(8,128)(2,1)S(1)}, u32[]{:S(2)}) copy-start(bf16[256,1,6,128]{0,3,2,1:T(8,128)(2,1)S(1)} %get-tuple-element.653) | copy-start | bytes 1179652 | tf_op jit(solution)/shard_map/while
  125.6 3.4 %copy-start.5 = (bf16[2048,128]{1,0:T(8,128)(2,1)S(1)}, bf16[2048,128]{1,0:T(8,128)(2,1)}, u32[]{:S(2)}) copy-start(bf16[2048,128]{1,0:T(8,128)(2,1)} %copy-done.4) | copy-start | bytes 1572868 | tf_op jit(solution)/shard_map/while
  126.5 2.5 %copy-start.3 = (bf16[256,1,6,128]{0,3,2,1:T(8,128)(2,1)S(1)}, bf16[256,1,6,128]{0,3,2,1:T(8,128)(2,1)}, u32[]{:S(2)}) copy-start(bf16[256,1,6,128]{0,3,2,1:T(8,128)(2,1)} %copy-done.2) | copy-start | bytes 1179652 | tf_op jit(solution)/shard_map/while
  129.0 0.8 copy-start.4
  129.0 5.2 %copy-start.2 = (bf16[256,1,6,128]{0,3,2,1:T(8,128)(2,1)}, bf16[256,1,6,128]{0,3,2,1:T(8,128)(2,1)S(1)}, u32[]{:S(2)}) copy-start(bf16[256,1,6,128]{0,3,2,1:T(8,128)(2,1)S(1)} %get-tuple-element.653) | copy-start | bytes 1179652 | tf_op jit(solution)/shard_map/while
  138.6 3.4 %copy-start.5 = (bf16[2048,128]{1,0:T(8,128)(2,1)S(1)}, bf16[2048,128]{1,0:T(8,128)(2,1)}, u32[]{:S(2)}) copy-start(bf16[2048,128]{1,0:T(8,128)(2,1)} %copy-done.4) | copy-start | bytes 1572868 | tf_op jit(solution)/shard_map/while
  139.4 2.5 %copy-start.3 = (bf16[256,1,6,128]{0,3,2,1:T(8,128)(2,1)S(1)}, bf16[256,1,6,128]{0,3,2,1:T(8,128)(2,1)}, u32[]{:S(2)}) copy-start(bf16[256,1,6,128]{0,3,2,1:T(8,128)(2,1)} %copy-done.2) | copy-start | bytes 1179652 | tf_op jit(solution)/shard_map/while
  142.0 0.8 copy-start.4
  142.0 5.2 %copy-start.2 = (bf16[256,1,6,128]{0,3,2,1:T(8,128)(2,1)}, bf16[256,1,6,128]{0,3,2,1:T(8,128)(2,1)S(1)}, u32[]{:S(2)}) copy-start(bf16[256,1,6,128]{0,3,2,1:T(8,128)(2,1)S(1)} %get-tuple-element.653) | copy-start | bytes 1179652 | tf_op jit(solution)/shard_map/while
  151.5 3.4 %copy-start.5 = (bf16[2048,128]{1,0:T(8,128)(2,1)S(1)}, bf16[2048,128]{1,0:T(8,128)(2,1)}, u32[]{:S(2)}) copy-start(bf16[2048,128]{1,0:T(8,128)(2,1)} %copy-done.4) | copy-start | bytes 1572868 | tf_op jit(solution)/shard_map/while
  152.3 2.5 %copy-start.3 = (bf16[256,1,6,128]{0,3,2,1:T(8,128)(2,1)S(1)}, bf16[256,1,6,128]{0,3,2,1:T(8,128)(2,1)}, u32[]{:S(2)}) copy-start(bf16[256,1,6,128]{0,3,2,1:T(8,128)(2,1)} %copy-done.2) | copy-start | bytes 1179652 | tf_op jit(solution)/shard_map/while
  154.9 0.8 copy-start.4
  154.9 5.2 %copy-start.2 = (bf16[256,1,6,128]{0,3,2,1:T(8,128)(2,1)}, bf16[256,1,6,128]{0,3,2,1:T(8,128)(2,1)S(1)}, u32[]{:S(2)}) copy-start(bf16[256,1,6,128]{0,3,2,1:T(8,128)(2,1)S(1)} %get-tuple-element.653) | copy-start | bytes 1179652 | tf_op jit(solution)/shard_map/while
  164.4 3.4 %copy-start.5 = (bf16[2048,128]{1,0:T(8,128)(2,1)S(1)}, bf16[2048,128]{1,0:T(8,128)(2,1)}, u32[]{:S(2)}) copy-start(bf16[2048,128]{1,0:T(8,128)(2,1)} %copy-done.4) | copy-start | bytes 1572868 | tf_op jit(solution)/shard_map/while
  165.3 2.5 %copy-start.3 = (bf16[256,1,6,128]{0,3,2,1:T(8,128)(2,1)S(1)}, bf16[256,1,6,128]{0,3,2,1:T(8,128)(2,1)}, u32[]{:S(2)}) copy-start(bf16[256,1,6,128]{0,3,2,1:T(8,128)(2,1)} %copy-done.2) | copy-start | bytes 1179652 | tf_op jit(solution)/shard_map/while
  167.8 39.5 %copy-start.1 = (f32[256,1,6,128]{0,3,2,1:T(8,128)S(1)}, f32[256,1,6,128]{0,3,2,1:T(8,128)}, u32[]{:S(2)}) copy-start(f32[256,1,6,128]{0,3,2,1:T(8,128)} %get-tuple-element.148) | copy-start | bytes 2359300
  169.4 9.6 %collective-permute-start.14 = (f32[256,256]{1,0:T(8,128)S(1)}, f32[256,256]{1,0:T(8,128)S(1)}, u32[]{:S(2)}, u32[]{:S(2)}) collective-permute-start(f32[256,256]{1,0:T(8,128)S(1)} %get-tuple-element.384), channel_id=1, source_target_pairs={{1,0},{2,1},{3,2},{4,3},{5,4},{6,5},{7,6},{8,7},{9,8},{10,9},{11,1... | collective-permute-start | bytes 786440 | tf_op jit(solution)/shard_map/ppermute | solution.py:20
  171.4 12.4 %collective-permute-start.15 = (f32[256,256]{1,0:T(8,128)S(1)}, f32[256,256]{1,0:T(8,128)S(1)}, u32[]{:S(2)}, u32[]{:S(2)}) collective-permute-start(f32[256,256]{1,0:T(8,128)S(1)} %get-tuple-element.389), channel_id=1, source_target_pairs={{2,0},{3,1},{4,2},{5,3},{6,4},{7,5},{8,6},{9,7},{10,8},{11,9},{12,... | collective-permute-start | bytes 786440 | tf_op jit(solution)/shard_map/ppermute | solution.py:20
  173.3 39.1 %collective-permute-start.16 = (f32[256,256]{1,0:T(8,128)S(1)}, f32[256,256]{1,0:T(8,128)S(1)}, u32[]{:S(2)}, u32[]{:S(2)}) collective-permute-start(f32[256,256]{1,0:T(8,128)S(1)} %get-tuple-element.388), channel_id=1, source_target_pairs={{3,0},{4,1},{5,2},{6,3},{7,4},{8,5},{9,6},{10,7},{11,8},{12,9},{13... | collective-permute-start | bytes 786440 | tf_op jit(solution)/shard_map/ppermute | solution.py:20
  175.2 37.2 %collective-permute-start.17 = (f32[256,256]{1,0:T(8,128)S(1)}, f32[256,256]{1,0:T(8,128)S(1)}, u32[]{:S(2)}, u32[]{:S(2)}) collective-permute-start(f32[256,256]{1,0:T(8,128)S(1)} %get-tuple-element.387), channel_id=1, source_target_pairs={{4,0},{5,1},{6,2},{7,3},{8,4},{9,5},{10,6},{11,7},{12,8},{13,9},{1... | collective-permute-start | bytes 786440 | tf_op jit(solution)/shard_map/ppermute | solution.py:20
  177.2 35.3 %collective-permute-start.18 = (f32[256,256]{1,0:T(8,128)S(1)}, f32[256,256]{1,0:T(8,128)}, u32[]{:S(2)}, u32[]{:S(2)}) collective-permute-start(f32[256,256]{1,0:T(8,128)S(1)} %get-tuple-element.386), channel_id=1, source_target_pairs={{5,0},{6,1},{7,2},{8,3},{9,4},{10,5},{11,6},{12,7},{13,8},{14,9},{... | collective-permute-start | bytes 786440 | tf_op jit(solution)/shard_map/ppermute | solution.py:20
  179.1 33.3 %collective-permute-start.19 = (f32[256,256]{1,0:T(8,128)S(1)}, f32[256,256]{1,0:T(8,128)}, u32[]{:S(2)}, u32[]{:S(2)}) collective-permute-start(f32[256,256]{1,0:T(8,128)S(1)} %get-tuple-element.385), channel_id=1, source_target_pairs={{6,0},{7,1},{8,2},{9,3},{10,4},{11,5},{12,6},{13,7},{14,8},{15,9},... | collective-permute-start | bytes 786440 | tf_op jit(solution)/shard_map/ppermute | solution.py:20
  183.8 28.7 %collective-permute-start.20 = (f32[256,256]{1,0:T(8,128)S(1)}, f32[256,256]{1,0:T(8,128)}, u32[]{:S(2)}, u32[]{:S(2)}) collective-permute-start(f32[256,256]{1,0:T(8,128)S(1)} %get-tuple-element.390), channel_id=1, source_target_pairs={{7,0},{8,1},{9,2},{10,3},{11,4},{12,5},{13,6},{14,7},{15,8},{16,9}... | collective-permute-start | bytes 786440 | tf_op jit(solution)/shard_map/ppermute | solution.py:20
  208.9 11.0 %all-to-all-start.4 = ((bf16[4,64,768]{2,1,0:T(8,128)(2,1)}), bf16[4,64,768]{2,1,0:T(8,128)(2,1)S(1)}, u32[]{:S(2)}, u32[]{:S(2)}) async-start(bf16[4,64,768]{2,1,0:T(8,128)(2,1)} %all_to_all.108), calls=%async_computation.4 | async-start | bytes 786432 | tf_op jit(solution)/shard_map/all_to_all | solution.py:160
  219.9 8.9 %all-to-all-start.6 = ((bf16[4,64,128]{2,1,0:T(8,128)(2,1)}), bf16[4,64,128]{2,1,0:T(8,128)(2,1)S(1)}, u32[]{:S(2)}, u32[]{:S(2)}) async-start(bf16[4,64,128]{2,1,0:T(8,128)(2,1)} %bitcast.12), calls=%async_computation.6 | async-start | bytes 131072 | tf_op jit(solution)/shard_map/all_to_all | solution.py:162
  228.8 8.9 %all-to-all-start.5 = ((bf16[4,64,128]{2,1,0:T(8,128)(2,1)}), bf16[4,64,128]{2,1,0:T(8,128)(2,1)S(1)}, u32[]{:S(2)}, u32[]{:S(2)}) async-start(bf16[4,64,128]{2,1,0:T(8,128)(2,1)} %bitcast.10), calls=%async_computation.5 | async-start | bytes 131072 | tf_op jit(solution)/shard_map/all_to_all | solution.py:161
where the time goes:
time: 241 us; the launch traced here: 238 us
  starting transfers between devices  114 us (47%)
  matrix products  44.6 us (19%)
  local copies, waits for them, and re-layouts  36.3 us (15%)
  waiting for transfers between devices  29 us (12%)
  other arithmetic  12.4 us (5%)
    ppermute x21, starting transfers between devices, shifted(): return lax.ppermute(value, axis, pairs)  86.6 us
    dot_general x8, matrix products, prob_grads_of(): jnp.einsum('rkgd,ckd->rkgc', grad_split, value_split, preferred_element_t...  12.7 us
    dot_general x8, matrix products, scores_of(): jnp.einsum('rkgd,ckd->rkgc', query_split, key_split, preferred_element_ty...  12 us
    dot_general x4, matrix products, grad_step(): jnp.einsum('rkgc,ckd->rkgd', score_grads, key_split, preferred_element_ty...  10.2 us
    dot_general x4, matrix products, grad_step(): jnp.einsum('rkgc,rkgd->ckd', probs_half, grad_split, preferred_element_ty...  7.27 us
    unnamed x22, local copies, waits for them, and re-layouts  6.02 us
    all_to_all x1, waiting for transfers between devices, body(): lax.all_to_all(query_out, 'head', split_axis=0, concat_axis=1, tiled=True)  5.51 us
    all_to_all x1, waiting for transfers between devices, body(): lax.all_to_all(out_grad, 'head', split_axis=1, concat_axis=0, tiled=True)  5.42 us
  transfers between devices with their start and end apart: 28, of which 8 were waited for; matrix products, arithmetic and copies ran while one was open for 8% of the time, Pallas kernels for 0%

commit v1 on v0

v1 whole, which is shorter than its diff:
```python
import functools

import jax
import jax.numpy as jnp
from jax import lax
from jax.experimental import pallas as pl
from jax.experimental.pallas import tpu as pltpu
from jax.sharding import PartitionSpec as P

HEAD_SIZE = 128
QUERY_HEADS = 24
KEY_VALUE_HEADS = 4
KINDS = 128
FAR = 1e30
LOG2_E = 1.4426950408889634
MESH = pl.DeviceIdType.MESH
CORES = 2

OTHER_2, SAME_2, OTHER_1, OTHER_3, EXTRA, SAME_3, SAME_1, SELF = range(8)
SLOTS = 8
CHIPS_BACK = {OTHER_2: 2, SAME_2: 2, OTHER_1: 1, OTHER_3: 3, SAME_3: 3, SAME_1: 1}


def kernel(
    sizes,
    q_in, k_in, v_in, g_in, seg_in,
    dq_out, dk_out, dv_out,
    seg, queries, grads, keys, values, keys_t, kinds, unkind,
    scores, pgrads, stats, ds_half, p_half, dq_t, dq_half,
    part, part_other, chain, shares, last,
    seg_sem, q_sem, g_sem, kv_sem, qg_send, kv_send, fwd_send, fwd_other_send,
    part_send, other_sem, chain_sem, share_sem, dq_send, dq_sem, last_send, last_sem,
):
    head_count, inner_count, outer_count, group = sizes
    head = lax.axis_index("head")
    inner = lax.axis_index("inner")
    outer = lax.axis_index("outer")
    core = outer % CORES
    per_inner = outer_count // CORES
    chips = inner_count * per_inner
    chip = inner * per_inner + outer // CORES
    shards = chips * CORES
    place = chip * CORES + core
    tokens = q_in.shape[0]
    rows = head_count * tokens

    def at_chip(step, on_core):
        to = (chip + step + chips) % chips
        return (head, to // per_inner, (to % per_inner) * CORES + on_core)

    def at_head(step):
        to = (head + step) % head_count
        return to, (to, inner, outer)

    def wait_for(ref, sem):
        pltpu.make_async_copy(ref, ref, sem).wait()

    def send(src, dst, send_sem, recv_sem, to):
        pltpu.make_async_remote_copy(
            src_ref=src, dst_ref=dst, send_sem=send_sem, recv_sem=recv_sem,
            device_id=to, device_id_type=MESH,
        ).start()

    other = at_chip(0, 1 - core)
    next_1, next_3 = at_chip(1, core), at_chip(3, core)
    back_1, back_3 = at_chip(-1, core), at_chip(-3, core)
    extra_to = at_chip(4 * core, 1 - core)
    extra_from = at_chip(-4 * (1 - core), 1 - core)

    load_seg = pltpu.make_async_copy(seg_in, seg, seg_sem)
    load_seg.start()

    barrier = pltpu.get_barrier_semaphore()
    partners = [at_head(step)[1] for step in range(1, head_count)]
    partners += [other, next_1, next_3, back_1, back_3]
    far = at_chip(8 * core - 4, 1 - core)
    for partner in partners + [far]:
        pl.semaphore_signal(barrier, inc=1, device_id=partner, device_id_type=MESH)
    pl.semaphore_wait(barrier, len(partners) + 1)

    mine = pl.ds(pl.multiple_of(head * tokens, tokens), tokens)

    def head_columns(number):
        return pl.ds(pl.multiple_of(number * HEAD_SIZE, HEAD_SIZE), HEAD_SIZE)

    for kind, (src, dst) in enumerate(((k_in, keys), (v_in, values))):
        for step in range(1, head_count):
            to, device = at_head(step)
            send(
                src.at[:, head_columns(to)], dst.at[SELF, mine, :],
                kv_send.at[kind], kv_sem.at[SELF, kind], device,
            )
        pltpu.make_async_copy(
            src.at[:, head_columns(head)], dst.at[SELF, mine, :], kv_sem.at[SELF, kind]
        ).start()

    def send_head(number, carry):
        target = pl.ds(pl.multiple_of(number * rows + head * tokens, tokens), tokens)
        for kind, (src, dst, sem) in enumerate(
            ((q_in, queries, q_sem), (g_in, grads, g_sem))
        ):
            for step in range(1, head_count):
                to, device = at_head(step)
                send(
                    src.at[:, head_columns(to * group + number)], dst.at[target, :],
                    qg_send.at[kind], sem.at[number], device,
                )
            pltpu.make_async_copy(
                src.at[:, head_columns(head * group + number)], dst.at[target, :], sem.at[number]
            ).start()
        return carry

    lax.fori_loop(0, group, send_head, 0)

    load_seg.wait()
    lanes = seg.shape[1]
    seg_rows = rows // lanes
    session = lax.broadcasted_iota(jnp.int32, (KINDS, lanes), 0)

    def shard_of(slot):
        if slot == SELF:
            return place
        if slot == EXTRA:
            return (place - 7 + 6 * core + shards) % shards
        on_core = core if slot in (SAME_1, SAME_2, SAME_3) else 1 - core
        return ((chip - CHIPS_BACK[slot] + chips) % chips) * CORES + on_core

    for slot in range(SLOTS):
        for part_row in range(seg_rows):
            ids = seg[pl.ds(shard_of(slot) * seg_rows + part_row, 1), :]
            ones = jnp.where(session == ids, 1.0, 0.0).astype(jnp.float32).T
            span = slice(part_row * lanes, (part_row + 1) * lanes)
            kinds[slot, span, :] = ones.astype(jnp.bfloat16)
            if slot == SELF:
                unkind[span, :] = ((ones - 1.0) * FAR).astype(jnp.bfloat16)

    def turn_keys(slot):
        keys_t[slot] = keys[slot].astype(jnp.float32).T.astype(jnp.bfloat16)

    both = ((0, keys), (1, values))
    for kind, array in both:
        wait_for(array.at[SELF], kv_sem.at[SELF, kind])
        for number, (slot, to) in enumerate(((SAME_1, next_1), (SAME_3, next_3), (EXTRA, extra_to))):
            send(
                array.at[SELF], array.at[slot],
                fwd_send.at[number, kind], kv_sem.at[slot, kind], to,
            )

    turn_keys(SELF)

    def hand_over(slot, slot_there, number, kind, array):
        send(
            array.at[slot], array.at[slot_there],
            fwd_other_send.at[number, kind], kv_sem.at[slot_there, kind], other,
        )

    for kind, array in both:
        for slot, slot_there, number, owner, to in (
            (SAME_1, OTHER_1, 0, 0, next_1),
            (SAME_3, OTHER_3, 1, 1, back_1),
        ):
            wait_for(array.at[slot], kv_sem.at[slot, kind])
            if kind == owner:
                send(
                    array.at[slot], array.at[SAME_2],
                    fwd_send.at[3, kind], kv_sem.at[SAME_2, kind], to,
                )
            hand_over(slot, slot_there, number, kind, array)
    turn_keys(SAME_1)
    turn_keys(SAME_3)
    for kind, array in both:
        wait_for(array.at[SAME_2], kv_sem.at[SAME_2, kind])
        hand_over(SAME_2, OTHER_2, 2, kind, array)
    turn_keys(SAME_2)
    for slot in (EXTRA, OTHER_1, OTHER_3, OTHER_2):
        for kind, array in both:
            wait_for(array.at[slot], kv_sem.at[slot, kind])
        turn_keys(slot)

    score_scale = HEAD_SIZE ** (-0.5)
    over_last = (((1,), (1,)), ((), ()))

    def folded(block):
        return block.reshape(rows // 8, 8, rows)

    def head_span(number):
        return pl.ds(pl.multiple_of(number * rows, rows), rows)

    def forward(number, carry):
        wait_for(queries.at[head_span(number), :], q_sem.at[number])
        wait_for(grads.at[head_span(number), :], g_sem.at[number])

        def products(slot):
            wide_keys = jnp.concatenate([keys[slot], kinds[slot]], axis=1)
            wide_queries = jnp.concatenate([queries[head_span(number), :], unkind[...]], axis=1)
            block = lax.dot_general(
                wide_keys, wide_queries, over_last, preferred_element_type=jnp.float32
            )
            pgrads[slot, number] = lax.dot_general(
                values[slot], grads[head_span(number), :], over_last,
                preferred_element_type=jnp.float32,
            )
            return block

        def top_of(slot, top):
            block = products(slot)
            scores[slot, number] = block
            return jnp.maximum(top, jnp.max(folded(block), axis=0))

        block = products(SELF)
        key_row = lax.broadcasted_iota(jnp.int32, (rows, rows), 0)
        query_column = lax.broadcasted_iota(jnp.int32, (rows, rows), 1)
        block = jnp.where(key_row <= query_column, block, -FAR)
        scores[SELF, number] = block
        top = lax.fori_loop(0, SELF, top_of, jnp.max(folded(block), axis=0))
        top = jnp.max(top, axis=0, keepdims=True) * (score_scale * LOG2_E)

        def sums_of(slot, carry):
            total, cross = carry
            weights = jnp.exp2(scores[slot, number] * (score_scale * LOG2_E) - top)
            scores[slot, number] = weights
            total = total + jnp.sum(folded(weights), axis=0)
            cross = cross + jnp.sum(folded(weights * pgrads[slot, number]), axis=0)
            return total, cross

        zeros = jnp.zeros((8, rows), jnp.float32)
        total, cross = lax.fori_loop(0, SLOTS, sums_of, (zeros, zeros))
        inverse = 1.0 / jnp.sum(total, axis=0, keepdims=True)
        stats[number, 0:1, :] = inverse
        stats[number, 1:2, :] = jnp.sum(cross, axis=0, keepdims=True) * inverse
        return carry

    lax.fori_loop(0, group, forward, 0)

    dq_t[...] = jnp.zeros_like(dq_t)

    def backward(slot, carry):
        for number in range(group):
            probs = scores[slot, number] * stats[number, 0:1, :]
            span = slice(number * rows, (number + 1) * rows)
            p_half[:, span] = probs.astype(jnp.bfloat16)
            ds_half[:, span] = (probs * (pgrads[slot, number] - stats[number, 1:2, :])).astype(
                jnp.bfloat16
            )
        dk = jnp.dot(ds_half[...], queries[...], preferred_element_type=jnp.float32)
        dv = jnp.dot(p_half[...], grads[...], preferred_element_type=jnp.float32)
        dq_t[...] += jnp.dot(keys_t[slot], ds_half[...], preferred_element_type=jnp.float32)

        @pl.when((slot != SELF) & (slot != SAME_1) & (slot != SAME_2) & (slot != SAME_3))
        def _():
            part[slot, 0] = dk.astype(jnp.bfloat16)
            part[slot, 1] = dv.astype(jnp.bfloat16)

        for here, number in ((OTHER_2, 2), (OTHER_1, 0), (OTHER_3, 1)):

            @pl.when(slot == here)
            def _():
                send(
                    part.at[here], part_other.at[number], part_send.at[here],
                    other_sem.at[number], other,
                )

        @pl.when(slot == EXTRA)
        def _():
            send(
                part.at[EXTRA], shares.at[2], part_send.at[EXTRA], share_sem.at[2], extra_from
            )

        @pl.when(slot == SAME_2)
        def _():
            wait_for(part_other.at[2], other_sem.at[2])
            part[SAME_2, 0] = (dk + part_other[2, 0].astype(jnp.float32)).astype(jnp.bfloat16)
            part[SAME_2, 1] = (dv + part_other[2, 1].astype(jnp.float32)).astype(jnp.bfloat16)
            send(
                part.at[SAME_2, 0], chain.at[0], part_send.at[SAME_2], chain_sem.at[0], back_1
            )
            send(
                part.at[SAME_2, 1], chain.at[1], part_send.at[SAME_2], chain_sem.at[1], next_1
            )

        for here, number, kind, to in ((SAME_3, 1, 1, back_3), (SAME_1, 0, 0, back_1)):

            @pl.when(slot == here)
            def _():
                wait_for(part_other.at[number], other_sem.at[number])
                wait_for(chain.at[kind], chain_sem.at[kind])
                sums = [
                    dk + part_other[number, 0].astype(jnp.float32),
                    dv + part_other[number, 1].astype(jnp.float32),
                ]
                sums[kind] = sums[kind] + chain[kind].astype(jnp.float32)
                part[here, 0] = sums[0].astype(jnp.bfloat16)
                part[here, 1] = sums[1].astype(jnp.bfloat16)
                send(
                    part.at[here], shares.at[number], part_send.at[here],
                    share_sem.at[number], to,
                )

        @pl.when(slot == SELF)
        def _():
            last[0] = dk
            last[1] = dv

        return carry

    lax.fori_loop(0, SLOTS, backward, 0)

    def send_back(number, carry):
        dq = dq_t[:, head_span(number)].T * score_scale
        dq_half[head_span(number), :] = dq.astype(jnp.bfloat16)
        columns = head_columns(head * group + number)
        for step in range(1, head_count):
            to, device = at_head(step)
            here = pl.ds(pl.multiple_of(number * rows + to * tokens, tokens), tokens)
            send(dq_half.at[here, :], dq_out.at[:, columns], dq_send, dq_sem, device)
        here = pl.ds(pl.multiple_of(number * rows + head * tokens, tokens), tokens)
        pltpu.make_async_copy(dq_half.at[here, :], dq_out.at[:, columns], dq_sem).start()
        return carry

    lax.fori_loop(0, group, send_back, 0)

    for number in (2, 1, 0):
        wait_for(shares.at[number], share_sem.at[number])
    own = head_columns(head)
    for kind, out in enumerate((dk_out, dv_out)):
        total = last[kind]
        for number in range(3):
            total = total + shares[number, kind].astype(jnp.float32)
        if kind == 0:
            total = total * score_scale
        part[SELF, kind] = total.astype(jnp.bfloat16)
        for step in range(1, head_count):
            to, device = at_head(step)
            here = pl.ds(pl.multiple_of(to * tokens, tokens), tokens)
            send(
                part.at[SELF, kind, here, :], out.at[:, own],
                last_send.at[kind], last_sem.at[kind], device,
            )
        pltpu.make_async_copy(
            part.at[SELF, kind, mine, :], out.at[:, own], last_sem.at[kind]
        ).start()

    peers = head_count - 1
    for kind, (src, kv) in enumerate(((q_in, k_in), (g_in, v_in))):
        wait_for(src.at[:, : peers * group * HEAD_SIZE], qg_send.at[kind])
        wait_for(kv.at[:, : peers * HEAD_SIZE], kv_send.at[kind])
        array = (keys, values)[kind]
        for number in range(4):
            wait_for(array.at[SELF], fwd_send.at[number, kind])
        for number in range(3):
            wait_for(array.at[SELF], fwd_other_send.at[number, kind])
        wait_for(part.at[SELF, kind, : peers * tokens, :], last_send.at[kind])
    for slot in range(SELF):
        wait_for(part.at[slot], part_send.at[slot])
    wait_for(dq_out.at[:, : peers * group * HEAD_SIZE], dq_send)
    wait_for(dq_out, dq_sem)
    wait_for(dk_out, last_sem.at[0])
    wait_for(dv_out, last_sem.at[1])


def body(query_heads, key_heads, value_matrix, out_grad, segment_ids):
    head_count = lax.axis_size("head")
    sizes = (head_count, lax.axis_size("inner"), lax.axis_size("outer"), query_heads.shape[1] // key_heads.shape[1])
    group = sizes[3]
    tokens = query_heads.shape[0]
    rows = head_count * tokens
    half, full = jnp.bfloat16, jnp.float32
    ids = segment_ids.reshape(-1, 128)
    dma = pltpu.SemaphoreType.DMA
    anywhere = pl.BlockSpec(memory_space=pl.ANY)
    return pl.pallas_call(
        functools.partial(kernel, sizes),
        out_shape=(
            jax.ShapeDtypeStruct(query_heads.shape, half),
            jax.ShapeDtypeStruct(key_heads.shape, half),
            jax.ShapeDtypeStruct(value_matrix.shape, half),
        ),
        in_specs=[anywhere] * 5,
        out_specs=[anywhere] * 3,
        scratch_shapes=[
            pltpu.VMEM(ids.shape, jnp.int32),
            pltpu.VMEM((group * rows, HEAD_SIZE), half),
            pltpu.VMEM((group * rows, HEAD_SIZE), half),
            pltpu.VMEM((SLOTS, rows, HEAD_SIZE), half),
            pltpu.VMEM((SLOTS, rows, HEAD_SIZE), half),
            pltpu.VMEM((SLOTS, HEAD_SIZE, rows), half),
            pltpu.VMEM((SLOTS, rows, KINDS), half),
            pltpu.VMEM((rows, KINDS), half),
            pltpu.VMEM((SLOTS, group, rows, rows), full),
            pltpu.VMEM((SLOTS, group, rows, rows), full),
            pltpu.VMEM((group, 8, rows), full),
            pltpu.VMEM((rows, group * rows), half),
            pltpu.VMEM((rows, group * rows), half),
            pltpu.VMEM((HEAD_SIZE, group * rows), full),
            pltpu.VMEM((group * rows, HEAD_SIZE), half),
            pltpu.VMEM((SLOTS, 2, rows, HEAD_SIZE), half),
            pltpu.VMEM((3, 2, rows, HEAD_SIZE), half),
            pltpu.VMEM((2, rows, HEAD_SIZE), half),
            pltpu.VMEM((3, 2, rows, HEAD_SIZE), half),
            pltpu.VMEM((2, rows, HEAD_SIZE), full),
            dma,
            dma((group,)),
            dma((group,)),
            dma((SLOTS, 2)),
            dma((2,)),
            dma((2,)),
            dma((4, 2)),
            dma((3, 2)),
            dma((SLOTS,)),
            dma((3,)),
            dma((2,)),
            dma((3,)),
            dma,
            dma,
            dma((2,)),
            dma((2,)),
        ],
        compiler_params=pltpu.CompilerParams(
            collective_id=0, has_side_effects=True, vmem_limit_bytes=56 * 2**20
        ),
    )(query_heads, key_heads, value_matrix, out_grad, ids)


def solution(mesh):
    split = P(("inner", "outer", "head"), None)
    return jax.shard_map(
        body,
        mesh=mesh,
        in_specs=(split, split, split, split, P()),
        out_specs=(split, split, split),
        check_vma=False,
    )
```

time: 241 us -> 70.3 us (0.29); the launches traced: 238 us -> 70.1 us
  starting transfers between devices: 114 us -> 0 us
  Pallas kernels: 0 us -> 66.2 us
  matrix products: 44.6 us -> 0 us
  local copies, waits for them, and re-layouts: 36.3 us -> 3.29 us
  waiting for transfers between devices: 29 us -> 0 us
  other arithmetic: 12.4 us -> 0 us
    ppermute x21 -> x0, starting transfers between devices: 86.6 us -> none  [shifted(): return lax.ppermute(value, axis, pairs)]
    pallas_call x0 -> x1, Pallas kernels: none -> 66.2 us  [body(): pl.pallas_call(functools.partial(kernel, sizes), out_shape=(jax.ShapeDtyp...]
    dot_general x28 -> x0, matrix products: 44.6 us -> none  [the longest x8 12.7 us: prob_grads_of(): jnp.einsum('rkgd,ckd->rkgc', grad_split, value_split, preferred_element_t...]
    all_to_all x7 -> x0, starting transfers between devices: 26.9 us -> none  [the longest x1 4.75 us: body(): lax.all_to_all(query_heads, 'head', split_axis=1, concat_axis=0, tiled=True)]
    all_to_all x7 -> x0, waiting for transfers between devices: 23.6 us -> none  [the longest x1 5.51 us: body(): lax.all_to_all(query_out, 'head', split_axis=0, concat_axis=1, tiled=True)]
    all_to_all x8 -> x0, local copies, waits for them, and re-layouts: 8.91 us -> none  [the longest x2 1.98 us: body(): lax.all_to_all(query_out, 'head', split_axis=0, concat_axis=1, tiled=True)]
    dynamic_slice x17 -> x0, local copies, waits for them, and re-layouts: 6.47 us -> none  [the longest x8 5.09 us: grad_step(): previous = lax.dynamic_slice_in_dim(pair_acc, offset, count, 0)]
    ppermute x21 -> x0, waiting for transfers between devices: 5.39 us -> none  [shifted(): return lax.ppermute(value, axis, pairs)]
  transfers between devices with their start and end apart: 28 -> 0, of which waited for: 8 -> 0; matrix products, arithmetic and copies ran while one was open for 8% -> 0% of each run, Pallas kernels for 0% -> 0%
where the time goes in v1:
time: 70.3 us; the launch traced here: 70.1 us
  Pallas kernels  66.2 us (94%)
  local copies, waits for them, and re-layouts  3.29 us (5%)
    pallas_call x1, Pallas kernels, body(): pl.pallas_call(functools.partial(kernel, sizes), out_shape=(jax.ShapeDtyp...  66.2 us
    unnamed x7, local copies, waits for them, and re-layouts  3.29 us

profile of v1, /device:TPU:32, one launch (start us, length us, event | category | flops | bytes accessed | tf_op | source)
XLA Modules:
  0.0 70.1 jit_solution(17525663112068802399)
XLA Ops:
  0.6 66.2 %shard_map.76 = (bf16[64,3072]{1,0:T(8,128)(2,1)}, bf16[64,512]{1,0:T(8,128)(2,1)}, bf16[64,512]{1,0:T(8,128)(2,1)}) custom-call(bf16[64,3072]{1,0:T(8,128)(2,1)} %q_in.1, bf16[64,512]{1,0:T(8,128)(2,1)} %k_in.1, bf16[64,512]{1,0:T(8,128)(2,1)} %v_in.1, bf16[64,3072]{1,0:T(8,128)(2,1)} %g_in.1, s32[128,128]{1,0:T(8,128)} %bitcast.1), custom_call_target="tpu_custom_call" | custom-call | tf_op jit(solution)/shard_map/pallas_call | solution.py:371
  66.8 0.0 copy-start.1
  66.8 1.8 %copy.11 = bf16[64,3072]{1,0:T(8,128)(2,1)} copy(bf16[64,3072]{1,0:T(8,128)(2,1)} %get-tuple-element.6) | data formatting | bytes 786432
  68.6 0.0 copy-done.1
  68.6 0.0 copy-start
  68.6 0.6 copy.12
  69.3 0.2 copy-done
  69.5 0.6 copy.13
Async XLA Ops:
  66.8 1.8 %copy-start.1 = (bf16[64,512]{1,0:T(8,128)(2,1)S(1)}, bf16[64,512]{1,0:T(8,128)(2,1)}, u32[]{:S(2)}) copy-start(bf16[64,512]{1,0:T(8,128)(2,1)} %get-tuple-element.7) | copy-start | bytes 196612
  68.6 0.9 %copy-start = (bf16[64,512]{1,0:T(8,128)(2,1)S(1)}, bf16[64,512]{1,0:T(8,128)(2,1)}, u32[]{:S(2)}) copy-start(bf16[64,512]{1,0:T(8,128)(2,1)} %get-tuple-element.8) | copy-start | bytes 196612

commit v2 on v1

v2 whole, which is shorter than its diff:
```python
import functools

import jax
import jax.numpy as jnp
from jax import lax
from jax.experimental import pallas as pl
from jax.experimental.pallas import tpu as pltpu
from jax.sharding import PartitionSpec as P

HEAD_SIZE = 128
QUERY_HEADS = 24
KEY_VALUE_HEADS = 4
KINDS = 128
FAR = 1e30
LOG2_E = 1.4426950408889634
MESH = pl.DeviceIdType.MESH
CORES = 2

SELF, SAME_1, SAME_3, EXTRA, SAME_2, OTHER_1, OTHER_3, OTHER_2 = range(8)
SLOTS = 8
CHIPS_BACK = {OTHER_2: 2, SAME_2: 2, OTHER_1: 1, OTHER_3: 3, SAME_3: 3, SAME_1: 1}
SHARES = 4
KEY, VALUE = range(2)


def kernel(
    sizes,
    q_in, k_in, v_in, g_in, seg_in,
    dq_out, shares,
    seg, queries, grads, keys, values, keys_t, kinds, unkind,
    scores, pgrads, tops, sums, crosses, ds_half, p_half, dq_t, dq_half,
    fresh, hold, part, part_other, chain,
    seg_sem, q_sem, g_sem, kv_sem, qg_send, kv_send, fwd_send, fwd_other_send,
    part_send, other_sem, chain_sem, share_sem, dq_send, dq_sem,
):
    head_count, inner_count, outer_count, group = sizes
    head = lax.axis_index("head")
    inner = lax.axis_index("inner")
    outer = lax.axis_index("outer")
    core = outer % CORES
    per_inner = outer_count // CORES
    chips = inner_count * per_inner
    chip = inner * per_inner + outer // CORES
    shards = chips * CORES
    place = chip * CORES + core
    tokens = q_in.shape[0]
    rows = head_count * tokens

    def at_chip(step, on_core):
        to = (chip + step + chips) % chips
        return (head, to // per_inner, (to % per_inner) * CORES + on_core)

    def at_head(step):
        to = (head + step) % head_count
        return to, (to, inner, outer)

    def wait_for(ref, sem):
        pltpu.make_async_copy(ref, ref, sem).wait()

    def send(src, dst, send_sem, recv_sem, to):
        pltpu.make_async_remote_copy(
            src_ref=src, dst_ref=dst, send_sem=send_sem, recv_sem=recv_sem,
            device_id=to, device_id_type=MESH,
        ).start()

    other = at_chip(0, 1 - core)
    next_1, next_3 = at_chip(1, core), at_chip(3, core)
    back_1, back_3 = at_chip(-1, core), at_chip(-3, core)
    extra_to = at_chip(4 * core, 1 - core)
    extra_from = at_chip(-4 * (1 - core), 1 - core)

    load_seg = pltpu.make_async_copy(seg_in, seg, seg_sem)
    load_seg.start()

    barrier = pltpu.get_barrier_semaphore()
    partners = [at_head(step)[1] for step in range(1, head_count)]
    partners += [other, next_1, next_3, back_1, back_3]
    far = at_chip(8 * core - 4, 1 - core)
    for partner in partners + [far]:
        pl.semaphore_signal(barrier, inc=1, device_id=partner, device_id_type=MESH)
    pl.semaphore_wait(barrier, len(partners) + 1)

    mine = pl.ds(pl.multiple_of(head * tokens, tokens), tokens)

    def head_columns(number):
        return pl.ds(pl.multiple_of(number * HEAD_SIZE, HEAD_SIZE), HEAD_SIZE)

    for kind, (src, dst) in enumerate(((k_in, keys), (v_in, values))):
        for step in range(1, head_count):
            to, device = at_head(step)
            send(
                src.at[:, head_columns(to)], dst.at[SELF, mine, :],
                kv_send.at[kind], kv_sem.at[SELF, kind], device,
            )
        pltpu.make_async_copy(
            src.at[:, head_columns(head)], dst.at[SELF, mine, :], kv_sem.at[SELF, kind]
        ).start()

    def send_head(number, carry):
        target = pl.ds(pl.multiple_of(number * rows + head * tokens, tokens), tokens)
        for kind, (src, dst, sem) in enumerate(
            ((q_in, queries, q_sem), (g_in, grads, g_sem))
        ):
            for step in range(1, head_count):
                to, device = at_head(step)
                send(
                    src.at[:, head_columns(to * group + number)], dst.at[target, :],
                    qg_send.at[kind], sem.at[number], device,
                )
            pltpu.make_async_copy(
                src.at[:, head_columns(head * group + number)], dst.at[target, :], sem.at[number]
            ).start()
        return carry

    lax.fori_loop(0, group, send_head, 0)

    load_seg.wait()
    lanes = seg.shape[1]
    seg_rows = rows // lanes
    session = lax.broadcasted_iota(jnp.int32, (KINDS, lanes), 0)

    def shard_of(slot):
        if slot == SELF:
            return place
        if slot == EXTRA:
            return (place - 7 + 6 * core + shards) % shards
        on_core = core if slot in (SAME_1, SAME_2, SAME_3) else 1 - core
        return ((chip - CHIPS_BACK[slot] + chips) % chips) * CORES + on_core

    for slot in range(SLOTS):
        for part_row in range(seg_rows):
            ids = seg[pl.ds(shard_of(slot) * seg_rows + part_row, 1), :]
            ones = jnp.where(session == ids, 1.0, 0.0).astype(jnp.float32).T
            span = slice(part_row * lanes, (part_row + 1) * lanes)
            kinds[slot, span, :] = ones.astype(jnp.bfloat16)
            if slot == SELF:
                unkind[span, :] = ((ones - 1.0) * FAR).astype(jnp.bfloat16)

    both = ((KEY, keys), (VALUE, values))
    onward = {SAME_1: (0, next_1), SAME_3: (1, next_3), EXTRA: (2, extra_to)}

    def pass_on(slot, kind):
        number, to = onward[slot]
        array = both[kind][1]
        send(
            array.at[SELF], array.at[slot],
            fwd_send.at[number, kind], kv_sem.at[slot, kind], to,
        )

    def arrived(slot, kind):
        wait_for(both[kind][1].at[slot], kv_sem.at[slot, kind])

    arrived(SELF, KEY)
    pass_on(SAME_1, KEY)
    arrived(SELF, VALUE)
    pass_on(SAME_3, VALUE)
    pass_on(SAME_1, VALUE)
    pass_on(SAME_3, KEY)
    pass_on(EXTRA, KEY)
    pass_on(EXTRA, VALUE)

    def hand_over(slot, slot_there, number, kind):
        array = both[kind][1]
        send(
            array.at[slot], array.at[slot_there],
            fwd_other_send.at[number, kind], kv_sem.at[slot_there, kind], other,
        )

    def relay(slot, kind, to):
        array = both[kind][1]
        send(
            array.at[slot], array.at[SAME_2], fwd_send.at[3, kind], kv_sem.at[SAME_2, kind], to
        )

    arrived(SAME_1, KEY)
    relay(SAME_1, KEY, next_1)
    hand_over(SAME_1, OTHER_1, 0, KEY)
    arrived(SAME_3, VALUE)
    relay(SAME_3, VALUE, back_1)
    hand_over(SAME_3, OTHER_3, 1, VALUE)
    arrived(SAME_1, VALUE)
    hand_over(SAME_1, OTHER_1, 0, VALUE)
    arrived(SAME_3, KEY)
    hand_over(SAME_3, OTHER_3, 1, KEY)

    score_scale = HEAD_SIZE ** (-0.5)
    exponent = score_scale * LOG2_E
    over_last = (((1,), (1,)), ((), ()))

    def folded(block):
        return block.reshape(rows // 8, 8, rows)

    def head_span(number):
        return pl.ds(pl.multiple_of(number * rows, rows), rows)

    def forward(slot, masked):
        keys_t[slot] = keys[slot].astype(jnp.float32).T.astype(jnp.bfloat16)
        wide_keys = jnp.concatenate([keys[slot], kinds[slot]], axis=1)
        for number in range(group):
            span = slice(number * rows, (number + 1) * rows)
            wide_queries = jnp.concatenate([queries[span, :], unkind[...]], axis=1)
            block = lax.dot_general(
                wide_keys, wide_queries, over_last, preferred_element_type=jnp.float32
            )
            if masked:
                key_row = lax.broadcasted_iota(jnp.int32, (rows, rows), 0)
                query_column = lax.broadcasted_iota(jnp.int32, (rows, rows), 1)
                block = jnp.where(key_row <= query_column, block, -FAR)
            slopes = lax.dot_general(
                values[slot], grads[span, :], over_last, preferred_element_type=jnp.float32
            )
            top = jnp.max(jnp.max(folded(block), axis=0), axis=0, keepdims=True)
            weights = jnp.exp2((block - top) * exponent)
            scores[slot, number] = weights
            pgrads[slot, number] = slopes
            here = pl.ds(slot, 1)
            tops[number, here, :] = top
            sums[number, here, :] = jnp.sum(
                jnp.sum(folded(weights), axis=0), axis=0, keepdims=True
            )
            crosses[number, here, :] = jnp.sum(
                jnp.sum(folded(weights * slopes), axis=0), axis=0, keepdims=True
            )

    for number in range(group):
        wait_for(queries.at[head_span(number), :], q_sem.at[number])
        wait_for(grads.at[head_span(number), :], g_sem.at[number])
    forward(SELF, True)

    def forward_next(slot, carry):
        @pl.when(slot == SAME_3)
        def _():
            for kind in (KEY, VALUE):
                arrived(SAME_2, kind)
                hand_over(SAME_2, OTHER_2, 2, kind)

        for late in (EXTRA, OTHER_1, OTHER_3, OTHER_2):

            @pl.when(slot == late)
            def _():
                for kind in (KEY, VALUE):
                    arrived(late, kind)

        forward(slot, False)
        return carry

    lax.fori_loop(SELF + 1, SLOTS, forward_next, 0)

    for number in range(group):
        top = tops[number]
        factor = jnp.exp2((top - jnp.max(top, axis=0, keepdims=True)) * exponent)
        total = jnp.sum(factor * sums[number], axis=0, keepdims=True)
        cross = jnp.sum(factor * crosses[number], axis=0, keepdims=True)
        tops[number] = factor / total
        sums[number, 0:1, :] = cross / total

    dq_t[...] = jnp.zeros_like(dq_t)

    def to_owners(slot, kind, number, step, on_core, first):
        for hop in range(first, head_count):
            to, _ = at_head(hop)
            here = pl.ds(pl.multiple_of(to * tokens, tokens), tokens)
            send(
                part.at[slot, kind, here, :], shares.at[number, head, kind],
                part_send.at[slot], share_sem, (to, *at_chip(step, on_core)[1:]),
            )

    def backward(turn, carry):
        slot = SLOTS - 1 - turn
        for number in range(group):
            span = slice(number * rows, (number + 1) * rows)
            probs = scores[slot, number] * tops[number, pl.ds(slot, 1), :]
            p_half[:, span] = probs.astype(jnp.bfloat16)
            ds_half[:, span] = (probs * (pgrads[slot, number] - sums[number, 0:1, :])).astype(
                jnp.bfloat16
            )
        fresh[KEY] = jnp.dot(ds_half[...], queries[...], preferred_element_type=jnp.float32)
        fresh[VALUE] = jnp.dot(p_half[...], grads[...], preferred_element_type=jnp.float32)
        part[slot] = fresh[...].astype(jnp.bfloat16)

        for here, number in ((OTHER_2, 2), (OTHER_3, 1), (OTHER_1, 0)):

            @pl.when(slot == here)
            def _():
                send(
                    part.at[here], part_other.at[number], part_send.at[here],
                    other_sem.at[number], other,
                )

        def add_other(here, kind, number):
            return fresh[kind] + part_other[number, kind].astype(jnp.float32)

        @pl.when(slot == SAME_2)
        def _():
            wait_for(part_other.at[2], other_sem.at[2])
            for kind, to in ((KEY, back_1), (VALUE, next_1)):
                part[SAME_2, kind] = add_other(SAME_2, kind, 2).astype(jnp.bfloat16)
                send(
                    part.at[SAME_2, kind], chain.at[kind], part_send.at[SAME_2],
                    chain_sem.at[kind], to,
                )

        @pl.when(slot == EXTRA)
        def _():
            for kind in (KEY, VALUE):
                to_owners(EXTRA, kind, 2, -4 * (1 - core), 1 - core, 0)

        for here, number, kind, step in ((SAME_3, 1, KEY, -3), (SAME_1, 0, VALUE, -1)):

            @pl.when(slot == here)
            def _():
                wait_for(part_other.at[number], other_sem.at[number])
                part[here, kind] = add_other(here, kind, number).astype(jnp.bfloat16)
                to_owners(here, kind, number, step, core, 0)
                hold[1 - kind] = add_other(here, 1 - kind, number)

        @pl.when(slot == SELF)
        def _():
            for kind in (KEY, VALUE):
                to_owners(SELF, kind, 3, 0, core, 1)
                pltpu.make_async_copy(
                    part.at[SELF, kind, mine, :], shares.at[3, head, kind], share_sem
                ).start()

        dq_t[...] += jnp.dot(keys_t[slot], ds_half[...], preferred_element_type=jnp.float32)
        return carry

    lax.fori_loop(0, SLOTS, backward, 0)

    for slot, kind, number, step in ((SAME_3, VALUE, 1, -3), (SAME_1, KEY, 0, -1)):
        wait_for(chain.at[kind], chain_sem.at[kind])
        part[slot, kind] = (hold[kind] + chain[kind].astype(jnp.float32)).astype(jnp.bfloat16)
        to_owners(slot, kind, number, step, core, 0)

    def send_back(number, carry):
        dq = dq_t[:, head_span(number)].T * score_scale
        dq_half[head_span(number), :] = dq.astype(jnp.bfloat16)
        columns = head_columns(head * group + number)
        for step in range(1, head_count):
            to, device = at_head(step)
            here = pl.ds(pl.multiple_of(number * rows + to * tokens, tokens), tokens)
            send(dq_half.at[here, :], dq_out.at[:, columns], dq_send, dq_sem, device)
        here = pl.ds(pl.multiple_of(number * rows + head * tokens, tokens), tokens)
        pltpu.make_async_copy(dq_half.at[here, :], dq_out.at[:, columns], dq_sem).start()
        return carry

    lax.fori_loop(0, group, send_back, 0)

    peers = head_count - 1
    for kind, (src, kv) in enumerate(((q_in, k_in), (g_in, v_in))):
        wait_for(src.at[:, : peers * group * HEAD_SIZE], qg_send.at[kind])
        wait_for(kv.at[:, : peers * HEAD_SIZE], kv_send.at[kind])
        array = (keys, values)[kind]
        for number in range(4):
            wait_for(array.at[SELF], fwd_send.at[number, kind])
        for number in range(3):
            wait_for(array.at[SELF], fwd_other_send.at[number, kind])
    for slot in range(SELF + 1, SLOTS):
        wait_for(part.at[slot], part_send.at[slot])
    wait_for(part.at[SELF, :, : peers * tokens, :], part_send.at[SELF])
    wait_for(dq_out.at[:, : peers * group * HEAD_SIZE], dq_send)
    wait_for(dq_out, dq_sem)
    wait_for(shares, share_sem)


def finish(dq_in, shares, dq_out, dk_out, dv_out):
    dq_out[...] = dq_in[...]
    heads = shares.shape[1]
    for kind, out in enumerate((dk_out, dv_out)):
        for head in range(heads):
            total = shares[0, head, kind].astype(jnp.float32)
            for number in range(1, SHARES):
                total = total + shares[number, head, kind].astype(jnp.float32)
            if kind == KEY:
                total = total * HEAD_SIZE ** (-0.5)
            out[:, head * HEAD_SIZE : (head + 1) * HEAD_SIZE] = total.astype(jnp.bfloat16)


def body(query_heads, key_heads, value_matrix, out_grad, segment_ids):
    head_count = lax.axis_size("head")
    sizes = (head_count, lax.axis_size("inner"), lax.axis_size("outer"), query_heads.shape[1] // key_heads.shape[1])
    group = sizes[3]
    tokens = query_heads.shape[0]
    rows = head_count * tokens
    half, full = jnp.bfloat16, jnp.float32
    ids = segment_ids.reshape(-1, 128)
    dma = pltpu.SemaphoreType.DMA
    anywhere = pl.BlockSpec(memory_space=pl.ANY)
    dq, shares = pl.pallas_call(
        functools.partial(kernel, sizes),
        out_shape=(
            jax.ShapeDtypeStruct(query_heads.shape, half),
            jax.ShapeDtypeStruct((SHARES, head_count, 2, tokens, HEAD_SIZE), half),
        ),
        in_specs=[anywhere] * 5,
        out_specs=[anywhere] * 2,
        scratch_shapes=[
            pltpu.VMEM(ids.shape, jnp.int32),
            pltpu.VMEM((group * rows, HEAD_SIZE), half),
            pltpu.VMEM((group * rows, HEAD_SIZE), half),
            pltpu.VMEM((SLOTS, rows, HEAD_SIZE), half),
            pltpu.VMEM((SLOTS, rows, HEAD_SIZE), half),
            pltpu.VMEM((SLOTS, HEAD_SIZE, rows), half),
            pltpu.VMEM((SLOTS, rows, KINDS), half),
            pltpu.VMEM((rows, KINDS), half),
            pltpu.VMEM((SLOTS, group, rows, rows), full),
            pltpu.VMEM((SLOTS, group, rows, rows), full),
            pltpu.VMEM((group, SLOTS, rows), full),
            pltpu.VMEM((group, SLOTS, rows), full),
            pltpu.VMEM((group, SLOTS, rows), full),
            pltpu.VMEM((rows, group * rows), half),
            pltpu.VMEM((rows, group * rows), half),
            pltpu.VMEM((HEAD_SIZE, group * rows), full),
            pltpu.VMEM((group * rows, HEAD_SIZE), half),
            pltpu.VMEM((2, rows, HEAD_SIZE), full),
            pltpu.VMEM((2, rows, HEAD_SIZE), full),
            pltpu.VMEM((SLOTS, 2, rows, HEAD_SIZE), half),
            pltpu.VMEM((3, 2, rows, HEAD_SIZE), half),
            pltpu.VMEM((2, rows, HEAD_SIZE), half),
            dma,
            dma((group,)),
            dma((group,)),
            dma((SLOTS, 2)),
            dma((2,)),
            dma((2,)),
            dma((4, 2)),
            dma((3, 2)),
            dma((SLOTS,)),
            dma((3,)),
            dma((2,)),
            dma,
            dma,
            dma,
        ],
        compiler_params=pltpu.CompilerParams(
            collective_id=0, has_side_effects=True, vmem_limit_bytes=56 * 2**20
        ),
    )(query_heads, key_heads, value_matrix, out_grad, ids)
    return pl.pallas_call(
        finish,
        out_shape=(
            jax.ShapeDtypeStruct(query_heads.shape, half),
            jax.ShapeDtypeStruct(key_heads.shape, half),
            jax.ShapeDtypeStruct(value_matrix.shape, half),
        ),
    )(dq, shares)


def solution(mesh):
    split = P(("inner", "outer", "head"), None)
    return jax.shard_map(
        body,
        mesh=mesh,
        in_specs=(split, split, split, split, P()),
        out_specs=(split, split, split),
        check_vma=False,
    )
```

time: 70.3 us -> 51.6 us (0.73)
  Pallas kernels: 66.2 us -> 50.8 us
  local copies, waits for them, and re-layouts: 3.29 us -> 0 us
    pallas_call x1, Pallas kernels: 66.2 us -> 48.8 us  [body(): pl.pallas_call(functools.partial(kernel, sizes), out_shape=(jax.ShapeDtyp...]
    unnamed x7 -> x0, local copies, waits for them, and re-layouts: 3.29 us -> none
    pallas_call x0 -> x1, Pallas kernels: none -> 1.98 us  [body(): pl.pallas_call(finish, out_shape=(jax.ShapeDtypeStruct(query_heads.shape,...]
where the time goes in v2:
time: 51.6 us; the launch traced here: 51.5 us
  Pallas kernels  50.8 us (98%)
  between operations  0.64 us (1%)
    pallas_call x1, Pallas kernels, body(): pl.pallas_call(functools.partial(kernel, sizes), out_shape=(jax.ShapeDtyp...  48.8 us
    pallas_call x1, Pallas kernels, body(): pl.pallas_call(finish, out_shape=(jax.ShapeDtypeStruct(query_heads.shape,...  1.98 us

profile of v2, /device:TPU:32, one launch (start us, length us, event | category | flops | bytes accessed | tf_op | source)
XLA Modules:
  0.0 51.5 jit_solution(7062536141042654417)
XLA Ops:
  0.6 48.8 %shard_map.76 = (bf16[64,3072]{1,0:T(8,128)(2,1)}, bf16[4,4,2,64,128]{4,3,2,1,0:T(8,128)(2,1)}) custom-call(bf16[64,3072]{1,0:T(8,128)(2,1)} %q_in.1, bf16[64,512]{1,0:T(8,128)(2,1)} %k_in.1, bf16[64,512]{1,0:T(8,128)(2,1)} %v_in.1, bf16[64,3072]{1,0:T(8,128)(2,1)} %g_in.1, s32[128,128]{1,0:T(8,128)} %bitcast.1), custom_call_target="tpu_custom_call" | custom-call | tf_op jit(solution)/shard_map/pallas_call | solution.py:389
  49.5 2.0 %shard_map.77 = (bf16[64,3072]{1,0:T(8,128)(2,1)}, bf16[64,512]{1,0:T(8,128)(2,1)}, bf16[64,512]{1,0:T(8,128)(2,1)}) custom-call(bf16[64,3072]{1,0:T(8,128)(2,1)} %get-tuple-element.5.dq_in, bf16[4,4,2,64,128]{4,3,2,1,0:T(8,128)(2,1)} %get-tuple-element.6.shares), custom_call_target="tpu_custom_call" | custom-call | tf_op jit(solution)/shard_map/pallas_call | solution.py:439

commit v3 on v2

--- a/solution.py
+++ b/solution.py
@@ -16,10 +16,11 @@
 MESH = pl.DeviceIdType.MESH
 CORES = 2
 
-SELF, SAME_1, SAME_3, EXTRA, SAME_2, OTHER_1, OTHER_3, OTHER_2 = range(8)
+OTHER_2, OTHER_3, OTHER_1, SELF, SAME_2, EXTRA, SAME_3, SAME_1 = range(8)
 SLOTS = 8
 CHIPS_BACK = {OTHER_2: 2, SAME_2: 2, OTHER_1: 1, OTHER_3: 3, SAME_3: 3, SAME_1: 1}
 SHARES = 4
+TOGETHER = 3
 KEY, VALUE = range(2)
 
 
@@ -28,7 +29,7 @@
     q_in, k_in, v_in, g_in, seg_in,
     dq_out, shares,
     seg, queries, grads, keys, values, keys_t, kinds, unkind,
-    scores, pgrads, tops, sums, crosses, ds_half, p_half, dq_t, dq_half,
+    scores, pgrads, tops, sums, crosses, ds_half, p_half, dq_half,
     fresh, hold, part, part_other, chain,
     seg_sem, q_sem, g_sem, kv_sem, qg_send, kv_send, fwd_send, fwd_other_send,
     part_send, other_sem, chain_sem, share_sem, dq_send, dq_sem,
@@ -172,62 +173,77 @@
             array.at[slot], array.at[SAME_2], fwd_send.at[3, kind], kv_sem.at[SAME_2, kind], to
         )
 
+    score_scale = HEAD_SIZE ** (-0.5)
+    exponent = score_scale * LOG2_E
+    over_last = (((1,), (1,)), ((), ()))
+
+    def folded(block):
+        return block.reshape(rows // 8, 8, block.shape[1])
+
+    def head_span(number):
+        return pl.ds(pl.multiple_of(number * rows, rows), rows)
+
+    def turn_keys(slot):
+        turned = keys[slot].astype(jnp.float32).T.astype(jnp.bfloat16)
+        if isinstance(slot, int):
+            keys_t[:, slot * rows : (slot + 1) * rows] = turned
+        else:
+            keys_t[:, head_span(slot)] = turned
+
+    def forward(slot, heads, masked):
+        wide_keys = jnp.concatenate([keys[slot], kinds[slot]], axis=1)
+        here = pl.ds(slot, 1)
+        for first in range(heads.start, heads.stop, TOGETHER):
+            count = min(TOGETHER, heads.stop - first)
+            span = slice(first * rows, (first + count) * rows)
+            wide_queries = jnp.concatenate(
+                [queries[span, :], jnp.concatenate([unkind[...]] * count, axis=0)], axis=1
+            )
+            block = lax.dot_general(
+                wide_keys, wide_queries, over_last, preferred_element_type=jnp.float32
+            )
+            if masked:
+                key_row = lax.broadcasted_iota(jnp.int32, (rows, rows), 0)
+                query_column = lax.broadcasted_iota(jnp.int32, (rows, rows), 1)
+                earlier = jnp.concatenate([key_row <= query_column] * count, axis=1)
+                block = jnp.where(earlier, block, -FAR)
+            slopes = lax.dot_general(
+                values[slot], grads[span, :], over_last, preferred_element_type=jnp.float32
+            )
+            top = jnp.max(jnp.max(folded(block), axis=0), axis=0, keepdims=True)
+            weights = jnp.exp2((block - top) * exponent)
+            scores[slot, :, span] = weights
+            pgrads[slot, :, span] = slopes
+            tops[here, span] = top
+            sums[here, span] = jnp.sum(jnp.sum(folded(weights), axis=0), axis=0, keepdims=True)
+            crosses[here, span] = jnp.sum(
+                jnp.sum(folded(weights * slopes), axis=0), axis=0, keepdims=True
+            )
+
+    def own_block(heads):
+        for number in heads:
+            wait_for(queries.at[head_span(number), :], q_sem.at[number])
+            wait_for(grads.at[head_span(number), :], g_sem.at[number])
+            forward(SELF, range(number, number + 1), True)
+
+    turn_keys(SELF)
+    own_block(range(0, group // 2))
     arrived(SAME_1, KEY)
     relay(SAME_1, KEY, next_1)
     hand_over(SAME_1, OTHER_1, 0, KEY)
     arrived(SAME_3, VALUE)
     relay(SAME_3, VALUE, back_1)
     hand_over(SAME_3, OTHER_3, 1, VALUE)
+    own_block(range(group // 2, group - 1))
     arrived(SAME_1, VALUE)
     hand_over(SAME_1, OTHER_1, 0, VALUE)
     arrived(SAME_3, KEY)
     hand_over(SAME_3, OTHER_3, 1, KEY)
-
-    score_scale = HEAD_SIZE ** (-0.5)
-    exponent = score_scale * LOG2_E
-    over_last = (((1,), (1,)), ((), ()))
-
-    def folded(block):
-        return block.reshape(rows // 8, 8, rows)
-
-    def head_span(number):
-        return pl.ds(pl.multiple_of(number * rows, rows), rows)
-
-    def forward(slot, masked):
-        keys_t[slot] = keys[slot].astype(jnp.float32).T.astype(jnp.bfloat16)
-        wide_keys = jnp.concatenate([keys[slot], kinds[slot]], axis=1)
-        for number in range(group):
-            span = slice(number * rows, (number + 1) * rows)
-            wide_queries = jnp.concatenate([queries[span, :], unkind[...]], axis=1)
-            block = lax.dot_general(
-                wide_keys, wide_queries, over_last, preferred_element_type=jnp.float32
-            )
-            if masked:
-                key_row = lax.broadcasted_iota(jnp.int32, (rows, rows), 0)
-                query_column = lax.broadcasted_iota(jnp.int32, (rows, rows), 1)
-                block = jnp.where(key_row <= query_column, block, -FAR)
-            slopes = lax.dot_general(
-                values[slot], grads[span, :], over_last, preferred_element_type=jnp.float32
-            )
-            top = jnp.max(jnp.max(folded(block), axis=0), axis=0, keepdims=True)
-            weights = jnp.exp2((block - top) * exponent)
-            scores[slot, number] = weights
-            pgrads[slot, number] = slopes
-            here = pl.ds(slot, 1)
-            tops[number, here, :] = top
-            sums[number, here, :] = jnp.sum(
-                jnp.sum(folded(weights), axis=0), axis=0, keepdims=True
-            )
-            crosses[number, here, :] = jnp.sum(
-                jnp.sum(folded(weights * slopes), axis=0), axis=0, keepdims=True
-            )
-
-    for number in range(group):
-        wait_for(queries.at[head_span(number), :], q_sem.at[number])
-        wait_for(grads.at[head_span(number), :], g_sem.at[number])
-    forward(SELF, True)
-
-    def forward_next(slot, carry):
+    own_block(range(group - 1, group))
+
+    def forward_next(turn, carry):
+        slot = SLOTS - 1 - turn - turn // 4
+
         @pl.when(slot == SAME_3)
         def _():
             for kind in (KEY, VALUE):
@@ -241,20 +257,18 @@
                 for kind in (KEY, VALUE):
                     arrived(late, kind)
 
-        forward(slot, False)
+        turn_keys(slot)
+        forward(slot, range(group), False)
         return carry
 
-    lax.fori_loop(SELF + 1, SLOTS, forward_next, 0)
-
-    for number in range(group):
-        top = tops[number]
-        factor = jnp.exp2((top - jnp.max(top, axis=0, keepdims=True)) * exponent)
-        total = jnp.sum(factor * sums[number], axis=0, keepdims=True)
-        cross = jnp.sum(factor * crosses[number], axis=0, keepdims=True)
-        tops[number] = factor / total
-        sums[number, 0:1, :] = cross / total
-
-    dq_t[...] = jnp.zeros_like(dq_t)
+    lax.fori_loop(0, SLOTS - 1, forward_next, 0)
+
+    top = tops[...]
+    factor = jnp.exp2((top - jnp.max(top, axis=0, keepdims=True)) * exponent)
+    total = jnp.sum(factor * sums[...], axis=0, keepdims=True)
+    cross = jnp.sum(factor * crosses[...], axis=0, keepdims=True)
+    tops[...] = factor / total
+    sums[0:1, :] = cross / total
 
     def to_owners(slot, kind, number, step, on_core, first):
         for hop in range(first, head_count):
@@ -265,16 +279,15 @@
                 part_send.at[slot], share_sem, (to, *at_chip(step, on_core)[1:]),
             )
 
-    def backward(turn, carry):
-        slot = SLOTS - 1 - turn
-        for number in range(group):
-            span = slice(number * rows, (number + 1) * rows)
-            probs = scores[slot, number] * tops[number, pl.ds(slot, 1), :]
+    def backward(slot, carry):
+        for first in range(0, group, TOGETHER):
+            span = slice(first * rows, min(first + TOGETHER, group) * rows)
+            probs = scores[slot, :, span] * tops[pl.ds(slot, 1), span]
             p_half[:, span] = probs.astype(jnp.bfloat16)
-            ds_half[:, span] = (probs * (pgrads[slot, number] - sums[number, 0:1, :])).astype(
+            ds_half[slot, :, span] = (probs * (pgrads[slot, :, span] - sums[0:1, span])).astype(
                 jnp.bfloat16
             )
-        fresh[KEY] = jnp.dot(ds_half[...], queries[...], preferred_element_type=jnp.float32)
+        fresh[KEY] = jnp.dot(ds_half[slot], queries[...], preferred_element_type=jnp.float32)
         fresh[VALUE] = jnp.dot(p_half[...], grads[...], preferred_element_type=jnp.float32)
         part[slot] = fresh[...].astype(jnp.bfloat16)
 
@@ -322,18 +335,13 @@
                     part.at[SELF, kind, mine, :], shares.at[3, head, kind], share_sem
                 ).start()
 
-        dq_t[...] += jnp.dot(keys_t[slot], ds_half[...], preferred_element_type=jnp.float32)
         return carry
 
     lax.fori_loop(0, SLOTS, backward, 0)
 
-    for slot, kind, number, step in ((SAME_3, VALUE, 1, -3), (SAME_1, KEY, 0, -1)):
-        wait_for(chain.at[kind], chain_sem.at[kind])
-        part[slot, kind] = (hold[kind] + chain[kind].astype(jnp.float32)).astype(jnp.bfloat16)
-        to_owners(slot, kind, number, step, core, 0)
-
     def send_back(number, carry):
-        dq = dq_t[:, head_span(number)].T * score_scale
+        blocks = ds_half[:, :, head_span(number)].reshape(SLOTS * rows, rows)
+        dq = jnp.dot(keys_t[...], blocks, preferred_element_type=jnp.float32).T * score_scale
         dq_half[head_span(number), :] = dq.astype(jnp.bfloat16)
         columns = head_columns(head * group + number)
         for step in range(1, head_count):
@@ -346,6 +354,11 @@
 
     lax.fori_loop(0, group, send_back, 0)
 
+    for slot, kind, number, step in ((SAME_3, VALUE, 1, -3), (SAME_1, KEY, 0, -1)):
+        wait_for(chain.at[kind], chain_sem.at[kind])
+        part[slot, kind] = (hold[kind] + chain[kind].astype(jnp.float32)).astype(jnp.bfloat16)
+        to_owners(slot, kind, number, step, core, 0)
+
     peers = head_count - 1
     for kind, (src, kv) in enumerate(((q_in, k_in), (g_in, v_in))):
         wait_for(src.at[:, : peers * group * HEAD_SIZE], qg_send.at[kind])
@@ -355,8 +368,9 @@
             wait_for(array.at[SELF], fwd_send.at[number, kind])
         for number in range(3):
             wait_for(array.at[SELF], fwd_other_send.at[number, kind])
-    for slot in range(SELF + 1, SLOTS):
-        wait_for(part.at[slot], part_send.at[slot])
+    for slot in range(SLOTS):
+        if slot != SELF:
+            wait_for(part.at[slot], part_send.at[slot])
     wait_for(part.at[SELF, :, : peers * tokens, :], part_send.at[SELF])
     wait_for(dq_out.at[:, : peers * group * HEAD_SIZE], dq_send)
     wait_for(dq_out, dq_sem)
@@ -400,17 +414,16 @@
             pltpu.VMEM((group * rows, HEAD_SIZE), half),
             pltpu.VMEM((SLOTS, rows, HEAD_SIZE), half),
             pltpu.VMEM((SLOTS, rows, HEAD_SIZE), half),
-            pltpu.VMEM((SLOTS, HEAD_SIZE, rows), half),
+            pltpu.VMEM((HEAD_SIZE, SLOTS * rows), half),
             pltpu.VMEM((SLOTS, rows, KINDS), half),
             pltpu.VMEM((rows, KINDS), half),
-            pltpu.VMEM((SLOTS, group, rows, rows), full),
-            pltpu.VMEM((SLOTS, group, rows, rows), full),
-            pltpu.VMEM((group, SLOTS, rows), full),
-            pltpu.VMEM((group, SLOTS, rows), full),
-            pltpu.VMEM((group, SLOTS, rows), full),
+            pltpu.VMEM((SLOTS, rows, group * rows), full),
+            pltpu.VMEM((SLOTS, rows, group * rows), full),
+            pltpu.VMEM((SLOTS, group * rows), full),
+            pltpu.VMEM((SLOTS, group * rows), full),
+            pltpu.VMEM((SLOTS, group * rows), full),
+            pltpu.VMEM((SLOTS, rows, group * rows), half),
             pltpu.VMEM((rows, group * rows), half),
-            pltpu.VMEM((rows, group * rows), half),
-            pltpu.VMEM((HEAD_SIZE, group * rows), full),
             pltpu.VMEM((group * rows, HEAD_SIZE), half),
             pltpu.VMEM((2, rows, HEAD_SIZE), full),
             pltpu.VMEM((2, rows, HEAD_SIZE), full),

time: 51.6 us -> 48.8 us (0.946); the launches traced: 51.5 us -> 48 us
  Pallas kernels: 50.8 us -> 47.4 us
    pallas_call x1, Pallas kernels: 48.8 us -> 45.4 us  [body(): pl.pallas_call(functools.partial(kernel, sizes), out_shape=(jax.ShapeDtyp...]
where the time goes in v3:
time: 48.8 us; the launch traced here: 48 us
  Pallas kernels  47.4 us (97%)
  between operations  0.64 us (1%)
    pallas_call x1, Pallas kernels, body(): pl.pallas_call(functools.partial(kernel, sizes), out_shape=(jax.ShapeDtyp...  45.4 us
    pallas_call x1, Pallas kernels, body(): pl.pallas_call(finish, out_shape=(jax.ShapeDtypeStruct(query_heads.shape,...  1.98 us

profile of v3, /device:TPU:32, one launch (start us, length us, event | category | flops | bytes accessed | tf_op | source)
XLA Modules:
  0.0 48.0 jit_solution(11066221792558756657)
XLA Ops:
  0.6 45.4 %shard_map.76 = (bf16[64,3072]{1,0:T(8,128)(2,1)}, bf16[4,4,2,64,128]{4,3,2,1,0:T(8,128)(2,1)}) custom-call(bf16[64,3072]{1,0:T(8,128)(2,1)} %q_in.1, bf16[64,512]{1,0:T(8,128)(2,1)} %k_in.1, bf16[64,512]{1,0:T(8,128)(2,1)} %v_in.1, bf16[64,3072]{1,0:T(8,128)(2,1)} %g_in.1, s32[128,128]{1,0:T(8,128)} %bitcast.1), custom_call_target="tpu_custom_call" | custom-call | tf_op jit(solution)/shard_map/pallas_call | solution.py:403
  46.0 2.0 %shard_map.77 = (bf16[64,3072]{1,0:T(8,128)(2,1)}, bf16[64,512]{1,0:T(8,128)(2,1)}, bf16[64,512]{1,0:T(8,128)(2,1)}) custom-call(bf16[64,3072]{1,0:T(8,128)(2,1)} %get-tuple-element.5.dq_in, bf16[4,4,2,64,128]{4,3,2,1,0:T(8,128)(2,1)} %get-tuple-element.6.shares), custom_call_target="tpu_custom_call" | custom-call | tf_op jit(solution)/shard_map/pallas_call | solution.py:452

commit v4 on v3

--- a/solution.py
+++ b/solution.py
@@ -244,7 +244,7 @@
     def forward_next(turn, carry):
         slot = SLOTS - 1 - turn - turn // 4
 
-        @pl.when(slot == SAME_3)
+        @pl.when(slot == EXTRA)
         def _():
             for kind in (KEY, VALUE):
                 arrived(SAME_2, kind)
@@ -279,7 +279,10 @@
                 part_send.at[slot], share_sem, (to, *at_chip(step, on_core)[1:]),
             )
 
-    def backward(slot, carry):
+    def only(condition):
+        return (lambda work: work()) if condition else (lambda work: None)
+
+    def backward(slot):
         for first in range(0, group, TOGETHER):
             span = slice(first * rows, min(first + TOGETHER, group) * rows)
             probs = scores[slot, :, span] * tops[pl.ds(slot, 1), span]
@@ -293,7 +296,7 @@
 
         for here, number in ((OTHER_2, 2), (OTHER_3, 1), (OTHER_1, 0)):
 
-            @pl.when(slot == here)
+            @only(slot == here)
             def _():
                 send(
                     part.at[here], part_other.at[number], part_send.at[here],
@@ -303,7 +306,7 @@
         def add_other(here, kind, number):
             return fresh[kind] + part_other[number, kind].astype(jnp.float32)
 
-        @pl.when(slot == SAME_2)
+        @only(slot == SAME_2)
         def _():
             wait_for(part_other.at[2], other_sem.at[2])
             for kind, to in ((KEY, back_1), (VALUE, next_1)):
@@ -313,21 +316,21 @@
                     chain_sem.at[kind], to,
                 )
 
-        @pl.when(slot == EXTRA)
+        @only(slot == EXTRA)
         def _():
             for kind in (KEY, VALUE):
                 to_owners(EXTRA, kind, 2, -4 * (1 - core), 1 - core, 0)
 
         for here, number, kind, step in ((SAME_3, 1, KEY, -3), (SAME_1, 0, VALUE, -1)):
 
-            @pl.when(slot == here)
+            @only(slot == here)
             def _():
                 wait_for(part_other.at[number], other_sem.at[number])
                 part[here, kind] = add_other(here, kind, number).astype(jnp.bfloat16)
                 to_owners(here, kind, number, step, core, 0)
                 hold[1 - kind] = add_other(here, 1 - kind, number)
 
-        @pl.when(slot == SELF)
+        @only(slot == SELF)
         def _():
             for kind in (KEY, VALUE):
                 to_owners(SELF, kind, 3, 0, core, 1)
@@ -335,9 +338,9 @@
                     part.at[SELF, kind, mine, :], shares.at[3, head, kind], share_sem
                 ).start()
 
-        return carry
-
-    lax.fori_loop(0, SLOTS, backward, 0)
+
+    for slot in (OTHER_2, OTHER_3, OTHER_1, SAME_2, SELF, EXTRA, SAME_3, SAME_1):
+        backward(slot)
 
     def send_back(number, carry):
         blocks = ds_half[:, :, head_span(number)].reshape(SLOTS * rows, rows)
@@ -352,7 +355,12 @@
         pltpu.make_async_copy(dq_half.at[here, :], dq_out.at[:, columns], dq_sem).start()
         return carry
 
-    lax.fori_loop(0, group, send_back, 0)
+    def send_some(turn, carry):
+        for one in range(3):
+            send_back(turn * 3 + one, carry)
+        return carry
+
+    lax.fori_loop(0, group // 3, send_some, 0)
 
     for slot, kind, number, step in ((SAME_3, VALUE, 1, -3), (SAME_1, KEY, 0, -1)):
         wait_for(chain.at[kind], chain_sem.at[kind])

time: 48.8 us -> 47.8 us (0.980); the launches traced: 48 us -> 47.6 us
  no operation moved by 1% of the time
where the time goes in v4:
time: 47.8 us; the launch traced here: 47.6 us
  Pallas kernels  47 us (98%)
  between operations  0.64 us (1%)
    pallas_call x1, Pallas kernels, body(): pl.pallas_call(functools.partial(kernel, sizes), out_shape=(jax.ShapeDtyp...  45 us
    pallas_call x1, Pallas kernels, body(): pl.pallas_call(finish, out_shape=(jax.ShapeDtypeStruct(query_heads.shape,...  1.98 us

profile of v4, /device:TPU:32, one launch (start us, length us, event | category | flops | bytes accessed | tf_op | source)
XLA Modules:
  0.0 47.6 jit_solution(13874201689558690347)
XLA Ops:
  0.6 45.0 %shard_map.76 = (bf16[64,3072]{1,0:T(8,128)(2,1)}, bf16[4,4,2,64,128]{4,3,2,1,0:T(8,128)(2,1)}) custom-call(bf16[64,3072]{1,0:T(8,128)(2,1)} %q_in.1, bf16[64,512]{1,0:T(8,128)(2,1)} %k_in.1, bf16[64,512]{1,0:T(8,128)(2,1)} %v_in.1, bf16[64,3072]{1,0:T(8,128)(2,1)} %g_in.1, s32[128,128]{1,0:T(8,128)} %bitcast.1), custom_call_target="tpu_custom_call" | custom-call | tf_op jit(solution)/shard_map/pallas_call | solution.py:411
  45.7 2.0 %shard_map.77 = (bf16[64,3072]{1,0:T(8,128)(2,1)}, bf16[64,512]{1,0:T(8,128)(2,1)}, bf16[64,512]{1,0:T(8,128)(2,1)}) custom-call(bf16[64,3072]{1,0:T(8,128)(2,1)} %get-tuple-element.5.dq_in, bf16[4,4,2,64,128]{4,3,2,1,0:T(8,128)(2,1)} %get-tuple-element.6.shares), custom_call_target="tpu_custom_call" | custom-call | tf_op jit(solution)/shard_map/pallas_call | solution.py:460

commit v5 on v4

--- a/solution.py
+++ b/solution.py
@@ -241,10 +241,11 @@
     hand_over(SAME_3, OTHER_3, 1, KEY)
     own_block(range(group - 1, group))
 
-    def forward_next(turn, carry):
-        slot = SLOTS - 1 - turn - turn // 4
-
-        @pl.when(slot == EXTRA)
+    def only(condition):
+        return (lambda work: work()) if condition else (lambda work: None)
+
+    def forward_next(slot):
+        @only(slot == EXTRA)
         def _():
             for kind in (KEY, VALUE):
                 arrived(SAME_2, kind)
@@ -252,16 +253,16 @@
 
         for late in (EXTRA, OTHER_1, OTHER_3, OTHER_2):
 
-            @pl.when(slot == late)
+            @only(slot == late)
             def _():
                 for kind in (KEY, VALUE):
                     arrived(late, kind)
 
         turn_keys(slot)
         forward(slot, range(group), False)
-        return carry
-
-    lax.fori_loop(0, SLOTS - 1, forward_next, 0)
+
+    for slot in (SAME_1, SAME_3, EXTRA, SAME_2, OTHER_1, OTHER_3, OTHER_2):
+        forward_next(slot)
 
     top = tops[...]
     factor = jnp.exp2((top - jnp.max(top, axis=0, keepdims=True)) * exponent)
@@ -278,9 +279,6 @@
                 part.at[slot, kind, here, :], shares.at[number, head, kind],
                 part_send.at[slot], share_sem, (to, *at_chip(step, on_core)[1:]),
             )
-
-    def only(condition):
-        return (lambda work: work()) if condition else (lambda work: None)
 
     def backward(slot):
         for first in range(0, group, TOGETHER):

time: 47.8 us -> 47.7 us (level)
  no operation moved by 1% of the time
where the time goes in v5:
time: 47.7 us; the launch traced here: 47.6 us
  Pallas kernels  46.9 us (98%)
  between operations  0.64 us (1%)
    pallas_call x1, Pallas kernels, body(): pl.pallas_call(functools.partial(kernel, sizes), out_shape=(jax.ShapeDtyp...  44.9 us
    pallas_call x1, Pallas kernels, body(): pl.pallas_call(finish, out_shape=(jax.ShapeDtypeStruct(query_heads.shape,...  1.98 us

profile of v5, /device:TPU:32, one launch (start us, length us, event | category | flops | bytes accessed | tf_op | source)
XLA Modules:
  0.0 47.6 jit_solution(6242670659974288813)
XLA Ops:
  0.6 44.9 %shard_map.76 = (bf16[64,3072]{1,0:T(8,128)(2,1)}, bf16[4,4,2,64,128]{4,3,2,1,0:T(8,128)(2,1)}) custom-call(bf16[64,3072]{1,0:T(8,128)(2,1)} %q_in.1, bf16[64,512]{1,0:T(8,128)(2,1)} %k_in.1, bf16[64,512]{1,0:T(8,128)(2,1)} %v_in.1, bf16[64,3072]{1,0:T(8,128)(2,1)} %g_in.1, s32[128,128]{1,0:T(8,128)} %bitcast.1), custom_call_target="tpu_custom_call" | custom-call | tf_op jit(solution)/shard_map/pallas_call | solution.py:409
  45.6 2.0 %shard_map.77 = (bf16[64,3072]{1,0:T(8,128)(2,1)}, bf16[64,512]{1,0:T(8,128)(2,1)}, bf16[64,512]{1,0:T(8,128)(2,1)}) custom-call(bf16[64,3072]{1,0:T(8,128)(2,1)} %get-tuple-element.5.dq_in, bf16[4,4,2,64,128]{4,3,2,1,0:T(8,128)(2,1)} %get-tuple-element.6.shares), custom_call_target="tpu_custom_call" | custom-call | tf_op jit(solution)/shard_map/pallas_call | solution.py:458
